TPU v7x, 128 devices: a whole 4x4x4 slice. The times are simulated.
128 devices in a mesh: dp: 8 (over z, core), proto: 16 (over x, y).
Axes of the slice: x: 4, y: 4, z: 4, core: 2. Of those that a mesh axis runs over, the one named last changes fastest.
Arguments:
- student_in: bfloat16 [4096, 1536], P(('dp', 'proto')), may hold values from -10 to 10
- teacher_in: bfloat16 [4096, 1536], P(('dp', 'proto')), may hold values from -10 to 10
- w1_student: bfloat16 [1536, 2048], P(None, 'proto'), may hold values from -0.15625 to 0.15625
- w2_student: bfloat16 [2048, 256], P('proto'), may hold values from -0.125 to 0.125
- w1_teacher: bfloat16 [1536, 2048], P(None, 'proto'), may hold values from -0.15625 to 0.15625
- w2_teacher: bfloat16 [2048, 256], P('proto'), may hold values from -0.125 to 0.125
- prototypes: bfloat16 [131072, 256], P(('dp', 'proto')), may hold values from -0.25 to 0.25
Outputs:
- grad_proto: float32 [131072, 256], P(('dp', 'proto'))
- grad_w1: float32 [1536, 2048], P(None, 'proto')
- grad_w2: float32 [2048, 256], P('proto')
- loss: float32 [], replicated
All inputs are finite; a program needn't handle non-finite values.
Results may differ from a plain program's by a relative error of at most 0.0008.
Values may be sent and summed in bfloat16 or wider, within the bound.
A program may use at most 128 MiB of HBM per device.

v0:
```python
import jax
import jax.numpy as jnp
from jax import lax
from jax.sharding import PartitionSpec as P

ITERS = 3


teacher_temp = 0.07
learner_sharpness = 0.1


def gelu_exact(values):
    return jax.nn.gelu(values, approximate=False)


def head_rows(rows_in, w_first, second_weight):
    pre = jnp.dot(rows_in, w_first, preferred_element_type=jnp.float32)
    hidden = gelu_exact(pre).astype(jnp.bfloat16)
    partial_raw = jnp.dot(hidden, second_weight, preferred_element_type=jnp.float32)
    return (pre, hidden, partial_raw)


def unit_scale(raw):
    return lax.rsqrt(jnp.sum(raw * raw, axis=1, keepdims=True) + 1e-06)


def similarity_matrix(unit, cluster_centers, temp):
    return (
        lax.dot_general(
            unit, cluster_centers, (((1,), (1,)), ((), ())), preferred_element_type=jnp.float32
        )
        / temp
    )


def balanced_target_loss(
    teach_unit,
    learner_direction,
    cluster_centers,
    image_views,
    total_protos,
    col_total,
    row_total,
    student_total,
):
    teach_logit = similarity_matrix(teach_unit, cluster_centers, teacher_temp)
    learner_score = similarity_matrix(learner_direction, cluster_centers, learner_sharpness)
    teach_exp = jnp.exp(teach_logit)
    weight_row = jnp.ones((teach_exp.shape[0],), jnp.float32)
    for sweep in range(ITERS):
        col_scale = 1.0 / (
            total_protos * col_total(jnp.sum(teach_exp * weight_row[:, None], axis=0))
        )
        row_sum = row_total(jnp.sum(teach_exp * col_scale[None, :], axis=1))
        weight_row = 1.0 / (image_views * row_sum)
    stud_total = student_total(jnp.sum(jnp.exp(learner_score), axis=1))
    log_norm = jnp.log(stud_total)
    assignment_labels = teach_exp * col_scale[None, :] / row_sum[:, None]
    learner_softmax = jnp.exp(learner_score - log_norm[:, None])
    score_derivative = (
        (learner_softmax - assignment_labels) / (image_views * learner_sharpness)
    ).astype(jnp.bfloat16)
    partial_loss = jnp.sum(assignment_labels * (log_norm[:, None] - learner_score))
    return (score_derivative, partial_loss)


def on_device(student_in, teacher_in, w1_student, w2_student, w1_teacher, w2_teacher, prototypes):
    devices = lax.axis_size("dp") * lax.axis_size("proto")
    image_views = student_in.shape[0] * devices
    total_protos = prototypes.shape[0] * devices
    stud_rows, teach_rows = (
        lax.all_gather(student_in, "proto", axis=0, tiled=True),
        lax.all_gather(teacher_in, "proto", axis=0, tiled=True),
    )
    stud_pre, stud_hidden, stud_part = head_rows(stud_rows, w1_student, w2_student)
    _, _, teach_part = head_rows(teach_rows, w1_teacher, w2_teacher)
    stud_raw, teacher_raw_logits = lax.psum((stud_part, teach_part), "proto")
    stud_scale = unit_scale(stud_raw)
    stud_float = stud_raw * stud_scale
    learner_direction = stud_float.astype(jnp.bfloat16)
    teach_unit = (teacher_raw_logits * unit_scale(teacher_raw_logits)).astype(jnp.bfloat16)
    cluster_centers = lax.all_gather(prototypes, "dp", axis=0, tiled=True)

    def col_total(values):
        return lax.psum(values, "dp")

    def row_total(values):
        return lax.psum(values, "proto")

    def student_total(values):
        return lax.psum(values, "proto")

    score_derivative, partial_loss = balanced_target_loss(
        teach_unit,
        learner_direction,
        cluster_centers,
        image_views,
        total_protos,
        col_total,
        row_total,
        student_total,
    )
    unit_part = jnp.dot(score_derivative, cluster_centers, preferred_element_type=jnp.float32)
    normalized_gradient = lax.psum(unit_part, "proto")
    grad_proto = lax.psum_scatter(
        lax.dot_general(
            score_derivative,
            learner_direction,
            (((0,), (0,)), ((), ())),
            preferred_element_type=jnp.float32,
        ),
        "dp",
        scatter_dimension=0,
        tiled=True,
    )
    loss = lax.psum(partial_loss, ("dp", "proto")) / image_views
    along = jnp.sum(stud_float * normalized_gradient, axis=1, keepdims=True)
    raw_grad = ((normalized_gradient - stud_float * along) * stud_scale).astype(jnp.bfloat16)
    local_w2 = lax.dot_general(
        stud_hidden, raw_grad, (((0,), (0,)), ((), ())), preferred_element_type=jnp.float32
    )
    hidden_grad = lax.dot_general(
        raw_grad, w2_student, (((1,), (1,)), ((), ())), preferred_element_type=jnp.float32
    )
    _, backward = jax.vjp(gelu_exact, stud_pre)
    pre_grad = backward(hidden_grad)[0].astype(jnp.bfloat16)
    local_w1 = lax.dot_general(
        stud_rows, pre_grad, (((0,), (0,)), ((), ())), preferred_element_type=jnp.float32
    )
    grad_w1, grad_w2 = lax.psum((local_w1, local_w2), "dp")
    return (grad_proto, grad_w1, grad_w2, loss)


def solution(mesh):
    placed = (
        P(("dp", "proto"), None),
        P(("dp", "proto"), None),
        P(None, "proto"),
        P("proto", None),
        P(None, "proto"),
        P("proto", None),
        P(("dp", "proto"), None),
    )
    return jax.shard_map(
        on_device,
        mesh=mesh,
        in_specs=placed,
        out_specs=(P(("dp", "proto"), None), P(None, "proto"), P("proto", None), P()),
        check_vma=False,
    )
```

profile of v0, /device:TPU:1, one launch (start us, length us, event | category | flops | bytes accessed | tf_op | source)
XLA Modules:
  0.0 664.7 jit_solution(6561817104415820184)
XLA Ops:
  9.5 47.6 %all-gather.4.cloned.1.call-done = bf16[512,1536]{1,0:T(8,128)(2,1)} async-done(((bf16[32,1536]{1,0:T(8,128)(2,1)}), bf16[512,1536]{1,0:T(8,128)(2,1)}) %all-gather.4.cloned.1.call-update) | async-done | bytes 1572880 | tf_op jit(solution)/shard_map/all_gather | solution.py:73
  57.1 3.1 multiply_convert_fusion.5
  60.9 1.8 fusion.93
  62.7 39.8 %all-gather.8.cloned.1.call-done = bf16[512,1536]{1,0:T(8,128)(2,1)} async-done(((bf16[32,1536]{1,0:T(8,128)(2,1)}), bf16[512,1536]{1,0:T(8,128)(2,1)}) %all-gather.8.cloned.1.call-update) | async-done | bytes 1572880 | tf_op jit(solution)/shard_map/all_gather | solution.py:74
  102.6 3.6 fusion.17
  106.8 85.4 %all-reduce.9.cloned.1.call-done = (f32[512,256]{1,0:T(8,128)}, f32[512,256]{1,0:T(8,128)}) async-done(((f32[512,256]{1,0:T(8,128)}, f32[512,256]{1,0:T(8,128)}), (f32[512,256]{1,0:T(8,128)}, f32[512,256]{1,0:T(8,128)})) %all-reduce.9.cloned.1.call-update) | async-done | bytes 1048592 | tf_op jit(solution)/shard_map/psum | solution.py:78
  193.4 1.2 multiply_reduce_fusion.8
  194.6 10.9 %fusion.88 = (f32[8192]{0:T(1024)S(1)}, f32[512,8192]{1,0:T(8,128)}) fusion(bf16[8192,256]{1,0:T(8,128)(2,1)} %all-gather.6.cloned.1.call-done, f32[512,256]{1,0:T(8,128)} %get-tuple-element.11, f32[512]{0:T(512)S(1)} %add_rsqrt_fusion), kind=kOutput, calls=%fused_computation.130 | convolution fusion | flops 2156126208 | bytes 21530624 | tf_op jit(solution)/shard_map/dot_general | solution.py:30
  205.6 22.9 %psum.94 = f32[8192]{0:T(1024)S(1)} all-reduce(f32[8192]{0:T(1024)S(1)} %get-tuple-element.20), channel_id=1, replica_groups=mesh['dp'=8,'proto'=16] {'dp'}, use_global_device_ids=true, to_apply=%region_7.0 | all-reduce | flops 8192 | bytes 65536 | tf_op jit(solution)/shard_map/psum | solution.py:86
  228.5 7.0 %multiply_reduce_fusion.4 = f32[512]{0:T(512)S(1)} fusion(f32[512,8192]{1,0:T(8,128)} %get-tuple-element.21, f32[8192]{0:T(1024)S(1)} %multiply_divide_fusion.3), kind=kLoop, calls=%fused_computation.5 | loop fusion | flops 8388096 | bytes 16812032 | tf_op jit(solution)/shard_map/reduce_sum | solution.py:55
  235.5 31.0 %psum.95 = f32[512]{0:T(512)S(1)} all-reduce(f32[512]{0:T(512)S(1)} %multiply_reduce_fusion.4), channel_id=1, replica_groups=mesh['dp'=8,'proto'=16] {'proto'}, use_global_device_ids=true, to_apply=%region_9.0 | all-reduce | flops 512 | bytes 4096 | tf_op jit(solution)/shard_map/psum | solution.py:89
  266.6 8.3 %multiply_reduce_fusion.3 = f32[8192]{0:T(1024)S(1)} fusion(f32[512,8192]{1,0:T(8,128)} %get-tuple-element.21, f32[512]{0:T(512)S(1)} %multiply_divide_fusion.5), kind=kLoop, calls=%fused_computation.4 | loop fusion | flops 8380416 | bytes 16812032 | tf_op jit(solution)/shard_map/reduce_sum | solution.py:53
  274.9 30.7 %psum.96 = f32[8192]{0:T(1024)S(1)} all-reduce(f32[8192]{0:T(1024)S(1)} %multiply_reduce_fusion.3), channel_id=1, replica_groups=mesh['dp'=8,'proto'=16] {'dp'}, use_global_device_ids=true, to_apply=%region_11.0 | all-reduce | flops 8192 | bytes 65536 | tf_op jit(solution)/shard_map/psum | solution.py:86
  305.6 7.0 %multiply_reduce_fusion.2 = f32[512]{0:T(512)S(1)} fusion(f32[512,8192]{1,0:T(8,128)} %get-tuple-element.21, f32[8192]{0:T(1024)S(1)} %multiply_divide_fusion.2), kind=kLoop, calls=%fused_computation.3 | loop fusion | flops 8388096 | bytes 16812032 | tf_op jit(solution)/shard_map/reduce_sum | solution.py:55
  312.6 28.7 %psum.97 = f32[512]{0:T(512)S(1)} all-reduce(f32[512]{0:T(512)S(1)} %multiply_reduce_fusion.2), channel_id=1, replica_groups=mesh['dp'=8,'proto'=16] {'proto'}, use_global_device_ids=true, to_apply=%region_13.0 | all-reduce | flops 512 | bytes 4096 | tf_op jit(solution)/shard_map/psum | solution.py:89
  341.3 8.4 %multiply_reduce_fusion.1 = f32[8192]{0:T(1024)S(1)} fusion(f32[512,8192]{1,0:T(8,128)} %get-tuple-element.21, f32[512]{0:T(512)S(1)} %multiply_divide_fusion.4), kind=kLoop, calls=%fused_computation.2 | loop fusion | flops 8380416 | bytes 16812032 | tf_op jit(solution)/shard_map/reduce_sum | solution.py:53
  349.6 30.6 %psum.98 = f32[8192]{0:T(1024)S(1)} all-reduce(f32[8192]{0:T(1024)S(1)} %multiply_reduce_fusion.1), channel_id=1, replica_groups=mesh['dp'=8,'proto'=16] {'dp'}, use_global_device_ids=true, to_apply=%region_15.0 | all-reduce | flops 8192 | bytes 65536 | tf_op jit(solution)/shard_map/psum | solution.py:86
  380.2 7.2 %multiply_reduce_fusion.5 = f32[512]{0:T(512)S(1)} fusion(f32[512,8192]{1,0:T(8,128)} %get-tuple-element.21, f32[8192]{0:T(1024)S(1)} %multiply_divide_fusion.1), kind=kLoop, calls=%fused_computation.9 | loop fusion | flops 8388096 | bytes 16812032 | tf_op jit(solution)/shard_map/reduce_sum | solution.py:55
  387.4 7.2 %exponential_reduce_fusion = (f32[512]{0:T(512)S(1)}, f32[512,8192]{1,0:T(8,128)}) fusion(bf16[8192,256]{1,0:T(8,128)(2,1)S(1)} %copy-done.3, f32[512,256]{1,0:T(8,128)S(1)} %copy-done.5, f32[512]{0:T(512)S(1)} %add_rsqrt_fusion.1), kind=kOutput, calls=%fused_computation.7 | convolution fusion | flops 2156133888 | bytes 21499904 | tf_op jit(solution)/shard_map/dot_general | solution.py:30
  394.6 30.4 %all-reduce = (f32[512]{0:T(512)S(1)}, f32[512]{0:T(512)S(1)}) all-reduce(f32[512]{0:T(512)S(1)} %get-tuple-element.18, f32[512]{0:T(512)S(1)} %multiply_reduce_fusion.5), channel_id=1, replica_groups=mesh['dp'=8,'proto'=16] {'proto'}, use_global_device_ids=true, to_apply=%region_3.0 | all-reduce | flops 1024 | bytes 8192 | tf_op jit(solution)/shard_map/psum | solution.py:92
  424.9 13.6 %multiply_reduce_fusion = (f32[]{:T(128)}, bf16[512,8192]{1,0:T(8,128)(2,1)S(1)}) fusion(f32[512,8192]{1,0:T(8,128)} %get-tuple-element.19, f32[512]{0:T(512)S(1)} %log.3, f32[512]{0:T(512)S(1)} %get-tuple-element.9, f32[512,8192]{1,0:T(8,128)} %get-tuple-element.21, f32[8192]{0:T(1024)S(1)} %multiply_divide_fusion.1), kind=kLoop, calls=%fused_computation | loop fusion | flops 41943040 | bytes 41979908 | tf_op jit(solution)/shard_map/reduce_sum | solution.py:64
  438.5 3.5 copy-done.2
  442.0 3.1 fusion.94
  445.2 87.1 %all-reduce.7.cloned.1.call-done = f32[512,256]{1,0:T(8,128)} async-done(((f32[512,256]{1,0:T(8,128)}), f32[512,256]{1,0:T(8,128)}) %all-reduce.7.cloned.1.call-update) | async-done | bytes 524304 | tf_op jit(solution)/shard_map/psum | solution.py:105
  532.4 1.3 multiply_reduce_fusion.6
  533.7 1.3 multiply_convert_fusion.1
  535.8 2.0 convolution_bitcast_fusion
  538.1 9.1 %fusion.85 = f32[8192,256]{1,0:T(8,128)} fusion(bf16[512,8192]{1,0:T(8,128)(2,1)} %copy-done.2, f32[512,256]{1,0:T(8,128)S(1)} %copy-done.5, f32[512]{0:T(512)S(1)} %add_rsqrt_fusion.1), kind=kOutput, calls=%fused_computation.128 | convolution fusion | flops 2147745792 | bytes 17303552 | tf_op jit(solution)/shard_map/dot_general | solution.py:107
  547.2 65.9 %psum.103 = f32[]{:T(128)} all-reduce(f32[]{:T(128)} %get-tuple-element.14), channel_id=1, replica_groups=mesh['dp'=8,'proto'=16] {'dp','proto'}, use_global_device_ids=true, to_apply=%region_24.0 | all-reduce | flops 1 | bytes 8 | tf_op jit(solution)/shard_map/psum | solution.py:117
  613.8 2.3 copy.11
  616.1 38.5 %reduce-scatter.2.cloned.1.call-done = f32[1024,256]{1,0:T(8,128)} async-done(((f32[8192,256]{1,0:T(8,128)}), f32[1024,256]{1,0:T(8,128)}) %reduce-scatter.2.cloned.1.call-update) | async-done | bytes 1048592 | tf_op jit(solution)/shard_map/reduce_scatter | solution.py:106
  654.6 1.6 copy.17
  (47 shorter events, 5.4 us)
Async XLA Ops:
  8.0 49.1 %copy-start = (bf16[1536,128]{1,0:T(8,128)(2,1)S(1)}, bf16[1536,128]{1,0:T(8,128)(2,1)}, u32[]{:S(2)}) copy-start(bf16[1536,128]{1,0:T(8,128)(2,1)} %param.9) | copy-start | bytes 1179652
  8.0 49.1 %all-gather.4.cloned.1.call-start = ((), (), s32[]{:S(2)}) async-start(), calls=%async_computation.1 | async-start | bytes 1671168 | tf_op jit(solution)/shard_map/all_gather | solution.py:73
  8.7 93.8 %all-gather.8.cloned.1.call-start = ((), (), s32[]{:S(2)}) async-start(), calls=%async_computation.3 | async-start | bytes 1671168 | tf_op jit(solution)/shard_map/all_gather | solution.py:74
  9.5 182.7 %all-reduce.9.cloned.1.call-start = ((), (), s32[]{:S(2)}) async-start(), calls=%async_computation.6 | async-start | bytes 2097152 | tf_op jit(solution)/shard_map/psum | solution.py:78
  60.2 0.7 copy-start.6
  106.2 88.5 %all-gather.6.cloned.1.call-start = ((), (), s32[]{:S(2)}) async-start(), calls=%async_computation.2 | async-start | bytes 4718592 | tf_op jit(solution)/shard_map/all_gather | solution.py:83
  106.7 425.6 %all-reduce.7.cloned.1.call-start = ((), (), s32[]{:S(2)}) async-start(), calls=%async_computation.5 | async-start | bytes 1048576 | tf_op jit(solution)/shard_map/psum | solution.py:105
  341.3 46.1 %copy-start.5 = (f32[512,256]{1,0:T(8,128)S(1)}, f32[512,256]{1,0:T(8,128)}, u32[]{:S(2)}) copy-start(f32[512,256]{1,0:T(8,128)} %get-tuple-element.10) | copy-start | bytes 1572868
  380.2 7.2 %copy-start.3 = (bf16[8192,256]{1,0:T(8,128)(2,1)S(1)}, bf16[8192,256]{1,0:T(8,128)(2,1)}, u32[]{:S(2)}) copy-start(bf16[8192,256]{1,0:T(8,128)(2,1)} %all-gather.6.cloned.1.call-done) | copy-start | bytes 12582916
  424.9 17.1 %copy-start.4 = (bf16[8192,256]{1,0:T(8,128)(2,1)S(1)}, bf16[8192,256]{1,0:T(8,128)(2,1)}, u32[]{:S(2)}) copy-start(bf16[8192,256]{1,0:T(8,128)(2,1)} %all-gather.6.cloned.1.call-done) | copy-start | bytes 12582916
  438.5 3.5 copy-start.2
  438.5 96.4 %copy-start.7 = (bf16[512,128]{1,0:T(8,128)(2,1)S(1)}, bf16[512,128]{1,0:T(8,128)(2,1)}, u32[]{:S(2)}) copy-start(bf16[512,128]{1,0:T(8,128)(2,1)} %copy-done.6) | copy-start | bytes 393220
  438.5 97.3 %copy-start.8 = (bf16[128,256]{1,0:T(8,128)(2,1)S(1)}, bf16[128,256]{1,0:T(8,128)(2,1)}, u32[]{:S(2)}) copy-start(bf16[128,256]{1,0:T(8,128)(2,1)} %param.10) | copy-start | bytes 196612
  438.5 97.3 %copy-start.9 = (bf16[512,1536]{1,0:T(8,128)(2,1)S(1)}, bf16[512,1536]{1,0:T(8,128)(2,1)}, u32[]{:S(2)}) copy-start(bf16[512,1536]{1,0:T(8,128)(2,1)} %all-gather.4.cloned.1.call-done) | copy-start | bytes 4718596
  438.5 97.3 %copy-start.10 = (f32[512,128]{1,0:T(8,128)S(1)}, f32[512,128]{1,0:T(8,128)}, u32[]{:S(2)}) copy-start(f32[512,128]{1,0:T(8,128)} %get-tuple-element.17) | copy-start | bytes 786436
  445.2 168.6 %all-reduce.11.cloned.1.call-start = ((), (), s32[]{:S(2)}) async-start(), calls=%async_computation.7 | async-start | bytes 1835008 | tf_op jit(solution)/shard_map/psum | solution.py:131
  537.8 118.4 %copy-start.1 = (bf16[1536,128]{1,0:T(8,128)(2,1)S(1)}, bf16[1536,128]{1,0:T(8,128)(2,1)}, u32[]{:S(2)}) copy-start(bf16[1536,128]{1,0:T(8,128)(2,1)} %param.9) | copy-start | bytes 1179652
  537.8 116.8 %reduce-scatter.2.cloned.1.call-start = ((), (), s32[]{:S(2)}) async-start(), calls=%async_computation.4 | async-start | bytes 9437184 | tf_op jit(solution)/shard_map/reduce_scatter | solution.py:106
Sparse Core Ops, SparseCore 0:
  11.0 46.0 all-gather.3
  59.3 43.1 all-gather.7
  106.4 85.7 all-reduce.8
  445.3 87.0 all-reduce.6
Sparse Core Ops, SparseCore 1:
  108.4 32.9 all-gather.5
  537.9 60.8 all-reduce.10
  601.6 53.0 reduce-scatter.1
where the time goes:
time: 665 us
  waiting for transfers between devices  301 us (45%)
  blocking collectives  240 us (36%)
  other arithmetic  56.4 us (8%)
  matrix products  41.7 us (6%)
  between operations  17.4 us (3%)
  local copies, waits for them, and re-layouts  8.09 us (1%)
    psum x1, waiting for transfers between devices, on_device(): normalized_gradient = lax.psum(unit_part, 'proto')  87.1 us
    psum x1, waiting for transfers between devices, on_device(): stud_raw, teacher_raw_logits = lax.psum((stud_part, teach_part), 'proto')  85.4 us
    psum x3, blocking collectives, col_total(): return lax.psum(values, 'dp')  84.2 us
    psum x1, blocking collectives, on_device(): loss = lax.psum(partial_loss, ('dp', 'proto')) / image_views  65.9 us
    psum x2, blocking collectives, row_total(): return lax.psum(values, 'proto')  59.7 us
    all_gather x1, waiting for transfers between devices, on_device(): lax.all_gather(student_in, 'proto', axis=0, tiled=True)  47.6 us
    all_gather x1, waiting for transfers between devices, on_device(): lax.all_gather(teacher_in, 'proto', axis=0, tiled=True)  39.8 us
    reduce_scatter x1, waiting for transfers between devices, on_device(): lax.psum_scatter(lax.dot_general(score_derivative, learner_direction, (((...  38.5 us
  transfers between devices with their start and end apart: 7, of which 5 were waited for; matrix products, arithmetic and copies ran while one was open for 3% of the time, Pallas kernels for 0%

commit v1 on v0

v1 whole, which is shorter than its diff:
```python
import functools
import math

import jax
import jax.numpy as jnp
from jax import lax
from jax.experimental import pallas as pl
from jax.experimental.pallas import tpu as pltpu
from jax.sharding import PartitionSpec as P

MESH = pl.DeviceIdType.MESH
TEACHER_TEMP = 0.07
STUDENT_TEMP = 0.1
LOG2E = 1.4426950408889634
LN2 = 0.6931471805599453
F32 = jnp.float32
BF16 = jnp.bfloat16


def normal_cdf(x):
    return 0.5 * (1.0 + lax.erf(x * (1.0 / math.sqrt(2.0))))


def gelu(x):
    return x * normal_cdf(x)


def gelu_slope(x):
    return normal_cdf(x) + x * (jnp.exp(-0.5 * x * x) * (1.0 / math.sqrt(2.0 * math.pi)))


def nt_dot(a, b):
    return lax.dot_general(a, b, (((1,), (1,)), ((), ())), preferred_element_type=F32)


def tn_dot(a, b):
    return lax.dot_general(a, b, (((0,), (0,)), ((), ())), preferred_element_type=F32)


def unit_scale(raw):
    return lax.rsqrt(jnp.sum(raw * raw, axis=1, keepdims=True) + 1e-06)


class Sems:
    def __init__(self):
        self.count = 0

    def take(self, n):
        base = self.count
        self.count += n
        return base


def kernel(dims, plan, s_in, t_in, w1s, w2s, w1t, w2t, protos, gp_out, gw1_out, gw2_out, loss_out, *scratch):
    nz, nx, ny, rb, q = dims["nz"], dims["nx"], dims["ny"], dims["rb"], dims["q"]
    ndp, npr = 2 * nz, nx * ny
    width, hb, cols, kp = w1s.shape[0], w1s.shape[1], w2s.shape[1], protos.shape[0]
    group = rb * npr
    crops = group * ndp
    total_protos = kp * ndp * npr
    tiles = crops // 128
    half = cols // 2
    (tok, pre_s, hid_s, rawp, rawr, unit, own_float, own_scale, ex, lg2, colb, wb, rows8, ps1, psa, psb, psbr, psc,
     gt, ptr, ugt, sibs, sibr, part, zrecv, precv, a2, a2r, b2, b2r, losst, lossr, lossd, lossdr, rg,
     gw, gwr, gwz, fw, ssem, rsem) = scratch
    units = unit

    dp, me = lax.axis_index("dp"), lax.axis_index("proto")
    z, c = dp // 2, dp % 2
    x, y = me // ny, me % ny

    def started(src, dst, sem, to_dp, to_proto):
        pltpu.make_async_remote_copy(
            src_ref=src, dst_ref=dst, send_sem=ssem.at[sem], recv_sem=rsem.at[sem],
            device_id=(to_dp, to_proto), device_id_type=MESH,
        ).start()

    def arrived(dst, sem):
        pltpu.make_async_copy(dst, dst, rsem.at[sem]).wait()

    def gone(src, sem):
        pltpu.make_async_copy(src, src, ssem.at[sem]).wait()

    def loop(lo, hi, fn):
        def step(k, carry):
            fn(k)
            return carry

        lax.fori_loop(lo, hi, step, 0)

    def proto_of(xx, yy):
        return lax.rem(xx + nx, nx) * ny + lax.rem(yy + ny, ny)

    def rows(p):
        return pl.ds(pl.multiple_of(p * rb, rb), rb)

    def ring(value, n):
        return lax.rem(value + n, n)

    barrier = pltpu.get_barrier_semaphore()

    def greet_proto(k):
        pl.semaphore_signal(barrier, inc=1, device_id=(dp, ring(me + k, npr)), device_id_type=MESH)

    def greet_dp(k):
        pl.semaphore_signal(barrier, inc=1, device_id=(ring(dp + k, ndp), me), device_id_type=MESH)

    loop(1, npr, greet_proto)
    loop(1, ndp, greet_dp)
    pl.semaphore_wait(barrier, npr - 1 + ndp - 1)

    inputs = (t_in, s_in)
    w1_of, w2_of = (w1t, w1s), (w2t, w2s)
    left, right = pl.ds(0, width // 2), pl.ds(width // 2, width // 2)
    lo, hi = pl.ds(0, half), pl.ds(half, half)
    sib = dp + 1 - 2 * c

    def tokens_start(v):
        tok[v, rows(me), :] = inputs[v][...]
        for k in range(1, nx):
            started(tok.at[v, rows(me)], tok.at[v, rows(me)], plan["tx"][v] + k, dp, proto_of(x + k, y))
        for k in range(1, ny):
            started(tok.at[v, rows(me)], tok.at[v, rows(me)], plan["ty"][v] + k, dp, proto_of(x, y + k))

    def tokens_forward(v):
        for k in range(1, max(nx, ny)):
            if k < nx:
                block = rows(proto_of(x - k, y))
                arrived(tok.at[v, block], plan["tx"][v] + k)
                for m in range(1, ny):
                    ref = tok.at[v, block, left]
                    started(ref, ref, plan["fa"][v] + k * ny + m, dp, proto_of(x, y + m))
            if k < ny:
                block = rows(proto_of(x, y - k))
                arrived(tok.at[v, block], plan["ty"][v] + k)
                for m in range(1, nx):
                    ref = tok.at[v, block, right]
                    started(ref, ref, plan["fb"][v] + k * nx + m, dp, proto_of(x + m, y))

    def tokens_wait(v):
        for k in range(1, nx):
            for m in range(1, ny):
                arrived(tok.at[v, rows(proto_of(x - k, y - m)), left], plan["fa"][v] + k * ny + m)
        for k in range(1, ny):
            for m in range(1, nx):
                arrived(tok.at[v, rows(proto_of(x - m, y - k)), right], plan["fb"][v] + k * nx + m)

    def tokens_drain(v):
        for k in range(1, nx):
            gone(tok.at[v, rows(me)], plan["tx"][v] + k)
            for m in range(1, ny):
                gone(tok.at[v, rows(proto_of(x - k, y)), left], plan["fa"][v] + k * ny + m)
        for k in range(1, ny):
            gone(tok.at[v, rows(me)], plan["ty"][v] + k)
            for m in range(1, nx):
                gone(tok.at[v, rows(proto_of(x, y - k)), right], plan["fb"][v] + k * nx + m)

    def head(v):
        step = min(group, 128)

        def chunk(i):
            r = pl.ds(pl.multiple_of(i * step, step), step)
            pre = jnp.dot(tok[v, r, :], w1_of[v][...], preferred_element_type=F32)
            hidden = gelu(pre).astype(BF16)
            if v == 1:
                pre_s[r, :] = pre
                hid_s[r, :] = hidden
            rawp[v, r, :] = jnp.dot(hidden, w2_of[v][...], preferred_element_type=F32)

        loop(0, group // step, chunk)

    def raw_send(v):
        def send(k):
            to = ring(me + k, npr)
            started(rawp.at[v, rows(to)], rawr.at[v, k], plan["rr"][v] + k, dp, to)

        loop(1, npr, send)

    def raw_finish(v):
        loop(1, npr, lambda k: arrived(rawr.at[v, k], plan["rr"][v] + k))
        raw = lax.fori_loop(1, npr, lambda k, s: s + rawr[v, k], rawp[v, rows(me), :])
        scale = unit_scale(raw)
        unit_float = raw * scale
        if v == 1:
            own_float[...] = unit_float
            own_scale[...] = scale
        units[v, z, c, rows(me), :] = unit_float.astype(BF16)

    def raw_drain(v):
        loop(1, npr, lambda k: gone(rawp.at[v, rows(ring(me + k, npr))], plan["rr"][v] + k))

    def ag_first(v):
        mine = units.at[v, z, c, rows(me)]
        loop(1, npr, lambda k: started(mine.at[:, lo], mine.at[:, lo], plan["a1"][v] + k, dp, ring(me + k, npr)))
        for k in range(1, nz):
            started(mine.at[:, hi], mine.at[:, hi], plan["b1"][v] + k, ring(z + k, nz) * 2 + c, me)

    def ag_second(v):
        for k in range(1, nz):
            arrived(units.at[v, ring(z - k, nz), c, rows(me), hi], plan["b1"][v] + k)
        col = units.at[v, :, c, rows(me), hi]
        loop(1, npr, lambda k: started(col, col, plan["b2"][v] + k, dp, ring(me + k, npr)))
        loop(1, npr, lambda k: arrived(units.at[v, z, c, rows(ring(me - k, npr)), lo], plan["a1"][v] + k))
        plane = units.at[v, z, c, :, lo]
        for k in range(1, nz):
            started(plane, plane, plan["a2"][v] + k, ring(z + k, nz) * 2 + c, me)
        started(plane, plane, plan["sa"][v], sib, me)

    def ag_third(v):
        for k in range(1, nz):
            plane = units.at[v, ring(z - k, nz), c, :, lo]
            arrived(plane, plan["a2"][v] + k)
            started(plane, plane, plan["sa"][v] + k, sib, me)
        loop(1, npr, lambda k: arrived(units.at[v, :, c, rows(ring(me - k, npr)), hi], plan["b2"][v] + k))
        whole = units.at[v, :, c, :, hi]
        started(whole, whole, plan["sb"][v], sib, me)

    def ag_wait(v):
        for k in range(nz):
            arrived(units.at[v, ring(z - k, nz), 1 - c, :, lo], plan["sa"][v] + k)
        arrived(units.at[v, :, 1 - c, :, hi], plan["sb"][v])

    def ag_drain(v):
        mine = units.at[v, z, c, rows(me)]
        loop(1, npr, lambda k: gone(mine.at[:, lo], plan["a1"][v] + k))
        loop(1, npr, lambda k: gone(units.at[v, :, c, rows(me), hi], plan["b2"][v] + k))
        for k in range(1, nz):
            gone(mine.at[:, hi], plan["b1"][v] + k)
            gone(units.at[v, z, c, :, lo], plan["a2"][v] + k)
        for k in range(nz):
            gone(units.at[v, ring(z - k, nz), c, :, lo], plan["sa"][v] + k)
        gone(units.at[v, :, c, :, hi], plan["sb"][v])

    pb = min(kp, 256)
    gtiles = group // 128

    def teacher_scores():
        colb[...] = jnp.zeros_like(colb)

        def step(i):
            g, b = i // (kp // pb), i % (kp // pb)
            r = pl.ds(pl.multiple_of(b * pb, pb), pb)
            s = nt_dot(protos[r, :], units[0, g // 2, g % 2])
            e = jnp.exp2(s * (LOG2E / TEACHER_TEMP))
            ex[r, pl.ds(pl.multiple_of(g * group, group), group)] = e
            acc = e[:, :128]
            for j in range(1, gtiles):
                acc = acc + e[:, j * 128 : (j + 1) * 128]
            colb[r, :] += acc

        loop(0, ndp * (kp // pb), step)

        def scale(i):
            r = pl.ds(pl.multiple_of(i * 64, 64), 64)
            total = jnp.sum(colb[r, :], axis=1, keepdims=True)
            colb[r, :] = jnp.broadcast_to(1.0 / (total_protos * total), (64, 128))

        loop(0, kp // 64, scale)

    def student_scores():
        rows8[...] = jnp.zeros_like(rows8)

        def step(i):
            g, b = i // (kp // pb), i % (kp // pb)
            r = pl.ds(pl.multiple_of(b * pb, pb), pb)
            cc = pl.ds(pl.multiple_of(g * group, group), group)
            s = nt_dot(protos[r, :], units[1, g // 2, g % 2]) * (LOG2E / STUDENT_TEMP)
            lg2[r, cc] = s
            e = jnp.exp2(s)
            rows8[:, cc] += jnp.sum(e.reshape(pb // 8, 8, group), axis=0)

        loop(0, ndp * (kp // pb), step)

    def row_pass(fresh):
        rows8[...] = jnp.zeros_like(rows8)

        def step(i):
            base = pl.multiple_of(i * 64, 64)
            if fresh:
                accs = [None] * 8
                for j in range(tiles):
                    lanes = slice(j * 128, (j + 1) * 128)
                    w = wb[0:8, lanes]
                    for a in range(8):
                        term = ex[pl.ds(base + 8 * a, 8), lanes] * w
                        accs[a] = term if accs[a] is None else accs[a] + term
                scales = []
                for a in range(8):
                    total = jnp.sum(accs[a], axis=1, keepdims=True)
                    scale = jnp.broadcast_to(1.0 / (total_protos * total), (8, 128))
                    colb[pl.ds(base + 8 * a, 8), :] = scale
                    scales.append(scale)
            else:
                scales = [colb[pl.ds(base + 8 * a, 8), :] for a in range(8)]
            for j in range(tiles):
                lanes = slice(j * 128, (j + 1) * 128)
                terms = [ex[pl.ds(base + 8 * a, 8), lanes] * scales[a] for a in range(8)]
                while len(terms) > 1:
                    terms = [terms[n] + terms[n + 1] for n in range(0, len(terms), 2)]
                rows8[:, lanes] += terms[0]

        loop(0, kp // 64, step)

    def put_rows(t, at):
        for j in range(tiles):
            ps1[t, j // q, at + j % q : at + j % q + 1, :] = jnp.sum(
                rows8[:, j * 128 : (j + 1) * 128], axis=0, keepdims=True
            )

    def sum_send(t):
        def send(k):
            to = ring(dp + k, ndp)
            started(ps1.at[t, to], psa.at[t, k], plan["s1"][t] + k, to, me)

        loop(1, ndp, send)

    def sum_middle(t):
        loop(1, ndp, lambda k: arrived(psa.at[t, k], plan["s1"][t] + k))
        total = ps1[t, dp]
        for k in range(1, ndp):
            total = total + psa[t, k]
        psb[t] = total
        loop(1, npr, lambda k: started(psb.at[t], psbr.at[t, k], plan["s2"][t] + k, dp, ring(me + k, npr)))

    def sum_last(t):
        loop(1, npr, lambda k: arrived(psbr.at[t, k], plan["s2"][t] + k))
        total = psb[t]
        for k in range(1, npr):
            total = total + psbr[t, k]
        psc[t, dp] = total
        loop(1, ndp, lambda k: started(psc.at[t, dp], psc.at[t, dp], plan["s3"][t] + k, ring(dp + k, ndp), me))

    def sum_wait(t):
        loop(1, ndp, lambda k: arrived(psc.at[t, ring(dp - k, ndp)], plan["s3"][t] + k))

    def sum_drain(t):
        loop(1, ndp, lambda k: gone(ps1.at[t, ring(dp + k, ndp)], plan["s1"][t] + k))
        loop(1, npr, lambda k: gone(psb.at[t], plan["s2"][t] + k))
        loop(1, ndp, lambda k: gone(psc.at[t, dp], plan["s3"][t] + k))

    def spread(t, at, fn, slot):
        for j in range(tiles):
            v = fn(psc[t, j // q, at + j % q : at + j % q + 1, :])
            wb[pl.ds(8 * slot, 8), j * 128 : (j + 1) * 128] = jnp.broadcast_to(v, (8, 128))

    ps1[...] = jnp.zeros_like(ps1)
    ptr[...] = protos[...].astype(F32).T.astype(BF16)
    tokens_start(0)
    tokens_forward(0)
    tokens_wait(0)
    head(0)
    raw_send(0)
    raw_finish(0)
    ag_first(0)
    ag_second(0)
    tokens_start(1)
    ag_third(0)
    ag_wait(0)
    teacher_scores()
    tokens_forward(1)
    row_pass(False)
    put_rows(0, 0)
    sum_send(0)
    tokens_wait(1)
    head(1)
    raw_send(1)
    sum_middle(0)
    raw_finish(1)
    ag_first(1)
    sum_last(0)
    ag_second(1)
    sum_wait(0)
    spread(0, 0, lambda v: 1.0 / (crops * v), 0)
    row_pass(True)
    put_rows(1, 0)
    sum_send(1)
    ag_third(1)
    sum_middle(1)
    ag_wait(1)
    sum_last(1)
    student_scores()
    put_rows(2, 4)
    sum_wait(1)
    spread(1, 0, lambda v: 1.0 / (crops * v), 0)
    row_pass(True)
    put_rows(2, 0)
    sum_send(2)
    sum_middle(2)
    sum_last(2)
    sum_wait(2)
    spread(2, 0, lambda v: 1.0 / v, 0)
    spread(2, 4, lambda v: jnp.log(v) * LOG2E, 1)

    gp_out[...] = jnp.zeros_like(gp_out)
    losst[...] = jnp.zeros_like(losst)
    share = 1.0 / (crops * STUDENT_TEMP)

    def group_grads(zz, cc):
        lane0 = pl.multiple_of((zz * 2 + cc) * group, group)
        u = units[1, zz, cc]

        def step(b):
            base = pl.multiple_of(b * pb, pb)
            r = pl.ds(base, pb)
            lossa = jnp.zeros((8, 128), F32)
            for j in range(gtiles):
                lanes = pl.ds(pl.multiple_of(lane0 + j * 128, 128), 128)
                inv, norm = wb[0:8, lanes], wb[8:16, lanes]
                for a in range(0, pb, 16):
                    outs = []
                    for h in (0, 8):
                        rr = pl.ds(base + a + h, 8)
                        tgt = ex[rr, lanes] * colb[rr, :] * inv
                        rel = lg2[rr, lanes] - norm
                        lossa = lossa - tgt * rel
                        outs.append((jnp.exp2(rel) - tgt) * share)
                    gt[pl.ds(base + a, 16), j * 128 : (j + 1) * 128] = jnp.concatenate(outs, axis=0).astype(BF16)
            losst[...] += lossa
            gp_out[r, :] += jnp.dot(gt[r, :], u, preferred_element_type=F32)

        loop(0, kp // pb, step)
        ugt[...] = jnp.dot(ptr[...], gt[...], preferred_element_type=F32)
        return ugt[...].T

    for k in range(nz):
        zz = ring(z + 1 + k, nz)
        sibs[k] = group_grads(zz, 1 - c)
        started(sibs.at[k], sibr.at[k], plan["g0"] + k, sib, me)
    for k in range(nz):
        zz = ring(z + 1 + k, nz)
        mine = group_grads(zz, c)
        arrived(sibr.at[k], plan["g0"] + k)
        part[zz] = mine + sibr[k]
        if k < nz - 1:
            started(part.at[zz, :, lo], zrecv.at[k], plan["gz"] + k, zz * 2 + c, me)

        def send(m, zz=zz):
            to = ring(me + m, npr)
            started(part.at[zz, rows(to), hi], precv.at[m, zz], plan["gp"] + m, dp, to)

        loop(1, npr, send)

    losst[...] = losst[...] * (LN2 / crops)
    loop(1, npr, lambda k: started(losst, lossr.at[k], plan["l1"] + k, dp, ring(me + k, npr)))

    total = part[z, :, lo]
    for k in range(nz - 1):
        arrived(zrecv.at[k], plan["gz"] + k)
        total = total + zrecv[k]
    a2[...] = total
    loop(1, npr, lambda k: started(a2.at[rows(ring(me + k, npr))], a2r.at[k], plan["ga"] + k, dp, ring(me + k, npr)))

    loop(1, npr, lambda k: arrived(precv.at[k], plan["gp"] + k))
    b2[...] = lax.fori_loop(1, npr, lambda k, s: s + precv[k], part[:, rows(me), hi])
    for k in range(1, nz):
        zz = ring(z + k, nz)
        started(b2.at[zz], b2r.at[k], plan["gb"] + k, zz * 2 + c, me)

    loop(1, npr, lambda k: arrived(lossr.at[k], plan["l1"] + k))
    lossd[...] = lax.fori_loop(1, npr, lambda k, s: s + lossr[k], losst[...])
    loop(1, ndp, lambda k: started(lossd, lossdr.at[k], plan["l2"] + k, ring(dp + k, ndp), me))

    loop(1, npr, lambda k: arrived(a2r.at[k], plan["ga"] + k))
    grad_lo = lax.fori_loop(1, npr, lambda k, s: s + a2r[k], a2[rows(me), :])
    grad_hi = b2[z]
    for k in range(1, nz):
        arrived(b2r.at[k], plan["gb"] + k)
        grad_hi = grad_hi + b2r[k]

    unit_grad = jnp.concatenate([grad_lo, grad_hi], axis=1)
    own = own_float[...]
    along = jnp.sum(own * unit_grad, axis=1, keepdims=True)
    rg[rows(me), :] = ((unit_grad - own * along) * own_scale[...]).astype(BF16)
    loop(1, npr, lambda k: started(rg.at[rows(me)], rg.at[rows(me)], plan["r1"] + k, dp, ring(me + k, npr)))
    loop(1, npr, lambda k: arrived(rg.at[rows(ring(me - k, npr))], plan["r1"] + k))

    raw_grad = rg[...]
    pre_grad = (nt_dot(raw_grad, w2s[...]) * gelu_slope(pre_s[...])).astype(BF16)
    w2g = tn_dot(hid_s[...], raw_grad)
    gw[pl.ds(width, hb), :] = w2g[:, :hb]
    gw[pl.ds(width + hb, hb), :] = w2g[:, hb:]
    wchunk = min(width, 256)
    for i in range(width // wchunk):
        sl = slice(i * wchunk, (i + 1) * wchunk)
        gw[sl, :] = tn_dot(tok[1, :, sl], pre_grad)

    whole = gw.shape[0]
    halfw, piece = whole // 2, whole // ndp

    def half_of(cc):
        return pl.ds(pl.multiple_of(cc * halfw, 8), halfw)

    def piece_of(zz):
        return pl.ds(pl.multiple_of(c * halfw + zz * piece, 8), piece)

    started(gw.at[half_of(1 - c)], gwr, plan["w0"], sib, me)
    arrived(gwr, plan["w0"])
    gw[half_of(c), :] += gwr[...]
    for k in range(1, nz):
        zz = ring(z + k, nz)
        started(gw.at[piece_of(zz)], gwz.at[k], plan["w1"] + k, zz * 2 + c, me)
    total = gw[piece_of(z), :]
    for k in range(1, nz):
        arrived(gwz.at[k], plan["w1"] + k)
        total = total + gwz[k]
    fw[piece_of(z), :] = total
    for k in range(1, nz):
        started(fw.at[piece_of(z)], fw.at[piece_of(z)], plan["w2"] + k, ring(z + k, nz) * 2 + c, me)
    for k in range(1, nz):
        arrived(fw.at[piece_of(ring(z - k, nz))], plan["w2"] + k)
    started(fw.at[half_of(c)], fw.at[half_of(c)], plan["w3"], sib, me)

    loop(1, ndp, lambda k: arrived(lossdr.at[k], plan["l2"] + k))
    loss = lax.fori_loop(1, ndp, lambda k, s: s + lossdr[k], lossd[...])
    loss_out[...] = jnp.sum(jnp.sum(loss, axis=0, keepdims=True), axis=1, keepdims=True)

    arrived(fw.at[half_of(1 - c)], plan["w3"])
    gw1_out[...] = fw[:width, :]
    gw2_out[:, :hb] = fw[width : width + hb, :]
    gw2_out[:, hb:] = fw[width + hb :, :]

    for v in (0, 1):
        tokens_drain(v)
        raw_drain(v)
        ag_drain(v)
    for t in range(3):
        sum_drain(t)
    for k in range(nz):
        gone(sibs.at[k], plan["g0"] + k)
    for k in range(nz - 1):
        gone(part.at[0, :, lo], plan["gz"] + k)
    loop(1, npr, lambda k: gone(precv.at[k], plan["gp"] + k))
    loop(1, npr, lambda k: gone(losst, plan["l1"] + k))
    loop(1, ndp, lambda k: gone(lossd, plan["l2"] + k))
    loop(1, npr, lambda k: gone(a2r.at[k], plan["ga"] + k))
    for k in range(1, nz):
        gone(b2r.at[k], plan["gb"] + k)
        gone(gwz.at[k], plan["w1"] + k)
        gone(gwz.at[k], plan["w2"] + k)
    loop(1, npr, lambda k: gone(rg.at[rows(me)], plan["r1"] + k))
    gone(gwr, plan["w0"])
    gone(gwr, plan["w3"])


def step(dims, s_in, t_in, w1s, w2s, w1t, w2t, protos):
    nz, nx, ny = dims["nz"], dims["nx"], dims["ny"]
    ndp, npr = 2 * nz, nx * ny
    rb, width = s_in.shape
    hb, cols = w2s.shape
    kp = protos.shape[0]
    group = rb * npr
    crops = group * ndp
    half = cols // 2
    dims = dict(dims, rb=rb, q=group // 128)

    sems = Sems()
    plan = {
        name: [sems.take(n) for _ in range(2)]
        for name, n in dict(
            tx=nx, ty=ny, fa=nx * ny, fb=nx * ny, rr=npr, a1=npr, a2=nz, b1=nz, b2=npr, sa=nz, sb=1
        ).items()
    }
    for name, n in dict(s1=ndp, s2=npr, s3=ndp).items():
        plan[name] = [sems.take(n) for _ in range(3)]
    for name, n in dict(
        g0=nz, gz=nz, gp=npr, ga=npr, gb=nz, l1=npr, l2=ndp, r1=npr, w0=1, w1=nz, w2=nz, w3=1
    ).items():
        plan[name] = sems.take(n)

    wrows = width + 2 * hb
    V = pltpu.VMEM
    scratch = [
        V((2, group, width), BF16),
        V((group, hb), F32),
        V((group, hb), BF16),
        V((2, group, cols), F32),
        V((2, npr, rb, cols), F32),
        V((2, nz, 2, group, cols), BF16),
        V((rb, cols), F32),
        V((rb, 1), F32),
        V((kp, crops), F32),
        V((kp, crops), F32),
        V((kp, 128), F32),
        V((16, crops), F32),
        V((8, crops), F32),
        V((3, ndp, 8, 128), F32),
        V((3, ndp, 8, 128), F32),
        V((3, 8, 128), F32),
        V((3, npr, 8, 128), F32),
        V((3, ndp, 8, 128), F32),
        V((kp, group), BF16),
        V((cols, kp), BF16),
        V((cols, group), F32),
        V((nz, group, cols), F32),
        V((nz, group, cols), F32),
        V((nz, group, cols), F32),
        V((nz - 1, group, half), F32),
        V((npr, nz, rb, half), F32),
        V((group, half), F32),
        V((npr, rb, half), F32),
        V((nz, rb, half), F32),
        V((nz, rb, half), F32),
        V((8, 128), F32),
        V((npr, 8, 128), F32),
        V((8, 128), F32),
        V((ndp, 8, 128), F32),
        V((group, cols), BF16),
        V((wrows, hb), F32),
        V((wrows // 2, hb), F32),
        V((nz, wrows // ndp, hb), F32),
        V((wrows, hb), F32),
        pltpu.SemaphoreType.DMA((sems.count,)),
        pltpu.SemaphoreType.DMA((sems.count,)),
    ]
    vmem = pl.BlockSpec(memory_space=pltpu.VMEM)
    gp, gw1, gw2, loss = pl.pallas_call(
        functools.partial(kernel, dims, plan),
        out_shape=(
            jax.ShapeDtypeStruct((kp, cols), F32),
            jax.ShapeDtypeStruct((width, hb), F32),
            jax.ShapeDtypeStruct((hb, cols), F32),
            jax.ShapeDtypeStruct((1, 1), F32),
        ),
        in_specs=[vmem] * 7,
        out_specs=(vmem,) * 4,
        scratch_shapes=scratch,
        compiler_params=pltpu.CompilerParams(
            collective_id=0, has_side_effects=True, vmem_limit_bytes=63 * 1024 * 1024
        ),
        cost_estimate=pl.CostEstimate(
            flops=8 * kp * crops * cols, bytes_accessed=4 * kp * cols * 4, transcendentals=2 * kp * crops
        ),
    )(s_in, t_in, w1s, w2s, w1t, w2t, protos)
    return gp, gw1, gw2, loss[0, 0]


def solution(mesh):
    ndp, npr = mesh.shape["dp"], mesh.shape["proto"]
    side = math.isqrt(npr)
    dims = dict(nz=ndp // 2, nx=side, ny=npr // side)
    both = P(("dp", "proto"), None)
    return jax.shard_map(
        functools.partial(step, dims),
        mesh=mesh,
        in_specs=(both, both, P(None, "proto"), P("proto", None), P(None, "proto"), P("proto", None), both),
        out_specs=(both, P(None, "proto"), P("proto", None), P()),
        check_vma=False,
    )
```

time: 665 us -> 195 us (0.29)
  waiting for transfers between devices: 301 us -> 0 us
  blocking collectives: 240 us -> 0 us
  Pallas kernels: 0 us -> 188 us
  other arithmetic: 56.4 us -> 0 us
  matrix products: 41.7 us -> 0 us
  between operations: 17.4 us -> 2.42 us
    psum x7 -> x0, blocking collectives: 240 us -> none  [the longest x3 84.2 us: col_total(): return lax.psum(values, 'dp')]
    pallas_call x0 -> x1, Pallas kernels: none -> 188 us  [step(): pl.pallas_call(functools.partial(kernel, dims, plan), out_shape=(jax.Shap...]
    psum x3 -> x0, waiting for transfers between devices: 173 us -> none  [the longest x1 87.1 us: on_device(): normalized_gradient = lax.psum(unit_part, 'proto')]
    all_gather x3 -> x0, waiting for transfers between devices: 87.5 us -> none  [the longest x1 47.6 us: on_device(): lax.all_gather(student_in, 'proto', axis=0, tiled=True)]
    reduce_sum x9 -> x0, other arithmetic: 55 us -> none  [the longest x3 21.2 us: balanced_target_loss(): row_sum = row_total(jnp.sum(teach_exp * col_scale[None, :], axis=1))]
    dot_general x9 -> x0, matrix products: 41.7 us -> none  [the longest x2 18.1 us: similarity_matrix(): lax.dot_general(unit, cluster_centers, (((1,), (1,)), ((), ())), preferre...]
    reduce_scatter x1 -> x0, waiting for transfers between devices: 38.5 us -> none  [on_device(): lax.psum_scatter(lax.dot_general(score_derivative, learner_direction, (((...]
  transfers between devices with their start and end apart: 7 -> 0, of which waited for: 5 -> 0; matrix products, arithmetic and copies ran while one was open for 3% -> 0% of each run, Pallas kernels for 0% -> 0%
where the time goes in v1:
time: 195 us; the launch traced here: 194 us
  Pallas kernels  188 us (96%)
  local copies, waits for them, and re-layouts  4.02 us (2%)
  between operations  2.42 us (1%)
    pallas_call x1, Pallas kernels, step(): pl.pallas_call(functools.partial(kernel, dims, plan), out_shape=(jax.Shap...  188 us
    unnamed x7, local copies, waits for them, and re-layouts  4.02 us

profile of v1, /device:TPU:1, one launch (start us, length us, event | category | flops | bytes accessed | tf_op | source)
XLA Modules:
  0.0 194.5 jit_solution(4854549739357046122)
XLA Ops:
  0.6 188.1 %shard_map.102 = (f32[1024,256]{1,0:T(8,128)}, f32[1536,128]{1,0:T(8,128)}, f32[128,256]{1,0:T(8,128)}, f32[1,1]{1,0:T(1,128)}) custom-call(bf16[32,1536]{1,0:T(8,128)(2,1)} %s_in.1, bf16[32,1536]{1,0:T(8,128)(2,1)} %t_in.1, bf16[1536,128]{1,0:T(8,128)(2,1)} %w1s.1, bf16[128,256]{1,0:T(8,128)(2,1)} %w2s.1, bf16[1536,128]{1,0:T(8,128)(2,1)} %w1t.1, ...), custom_call_target="tpu_custom_call" | custom-call | flops 8589934592 | bytes 4194304 | tf_op jit(solution)/shard_map/pallas_call | solution.py:616
  188.7 0.0 copy-start
  188.7 2.3 %copy.15 = f32[1024,256]{1,0:T(8,128)} copy(f32[1024,256]{1,0:T(8,128)} %get-tuple-element.16) | data formatting | bytes 2097152
  191.0 0.0 copy-done
  191.0 0.0 copy-start.1
  191.1 0.9 copy.16
  191.9 0.1 copy-done.1
  192.1 0.7 copy.17
Async XLA Ops:
  188.7 2.3 %copy-start = (f32[1536,128]{1,0:T(8,128)S(1)}, f32[1536,128]{1,0:T(8,128)}, u32[]{:S(2)}) copy-start(f32[1536,128]{1,0:T(8,128)} %get-tuple-element.17) | copy-start | bytes 2359300
  191.0 1.0 copy-start.1

commit v2 on v1

v2 whole, which is shorter than its diff:
```python
import functools
import math

import jax
import jax.numpy as jnp
from jax import lax
from jax.experimental import pallas as pl
from jax.experimental.pallas import tpu as pltpu
from jax.sharding import PartitionSpec as P

MESH = pl.DeviceIdType.MESH
TEACHER_TEMP = 0.07
STUDENT_TEMP = 0.1
LOG2E = 1.4426950408889634
LN2 = 0.6931471805599453
F32 = jnp.float32
BF16 = jnp.bfloat16


def normal_cdf(x):
    return 0.5 * (1.0 + lax.erf(x * (1.0 / math.sqrt(2.0))))


def gelu(x):
    return x * normal_cdf(x)


def gelu_slope(x):
    return normal_cdf(x) + x * (jnp.exp(-0.5 * x * x) * (1.0 / math.sqrt(2.0 * math.pi)))


def nt_dot(a, b):
    return lax.dot_general(a, b, (((1,), (1,)), ((), ())), preferred_element_type=F32)


def tn_dot(a, b):
    return lax.dot_general(a, b, (((0,), (0,)), ((), ())), preferred_element_type=F32)


def unit_scale(raw):
    return lax.rsqrt(jnp.sum(raw * raw, axis=1, keepdims=True) + 1e-06)


def kernel(dims, plan, s_in, t_in, w1s_in, w2s_in, w1t_in, w2t_in, protos_in, gp_out, gw1_out, gw2_out, loss_out, *scratch):
    nz, nx, ny, rb, q = dims["nz"], dims["nx"], dims["ny"], dims["rb"], dims["q"]
    ndp, npr = 2 * nz, nx * ny
    width, hb, cols, kp = w1s_in.shape[0], w1s_in.shape[1], w2s_in.shape[1], protos_in.shape[0]
    group = rb * npr
    crops = group * ndp
    total_protos = kp * ndp * npr
    tiles = crops // 128
    part_rows = max(8, tiles)
    half = cols // 2
    (w1s, w2s, w1t, w2t, protos, tok, pre_s, hid_s, rawp, rawr, units, own_float, own_scale, ex, lg2, colb, wb, rows8,
     ps1, psa, psb, psbr, psc, gt, ptr, ugt, sibs, sibr, part, zrecv, precv, a2, a2r, b2, b2r, losst, lossr, lossd,
     lossdr, rg, gw, gwr, gwz, fw, ssem, rsem, lsem) = scratch

    dp, me = lax.axis_index("dp"), lax.axis_index("proto")
    z, c = dp // 2, dp % 2
    x, y = me // ny, me % ny

    def started(src, dst, name, to_dp, to_proto, nth=0):
        s, r = plan[name]
        pltpu.make_async_remote_copy(
            src_ref=src, dst_ref=dst, send_sem=ssem.at[s], recv_sem=rsem.at[r + nth],
            device_id=(to_dp, to_proto), device_id_type=MESH,
        ).start()

    def arrived(dst, name, nth=0):
        pltpu.make_async_copy(dst, dst, rsem.at[plan[name][1] + nth]).wait()

    def gone(src, name):
        pltpu.make_async_copy(src, src, ssem.at[plan[name][0]]).wait()

    def loop(lo, hi, fn, unroll=1):
        def step(k, carry):
            fn(k)
            return carry

        lax.fori_loop(lo, hi, step, 0, unroll=unroll)

    def proto_of(xx, yy):
        return lax.rem(xx + nx, nx) * ny + lax.rem(yy + ny, ny)

    def rows(p):
        return pl.ds(pl.multiple_of(p * rb, rb), rb)

    def ring(value, n):
        return lax.rem(value + n, n)

    inputs = (t_in, s_in)
    w1_of, w2_of = (w1t, w1s), (w2t, w2s)
    left, right = pl.ds(0, width // 2), pl.ds(width // 2, width // 2)
    lo, hi = pl.ds(0, half), pl.ds(half, half)
    sib = dp + 1 - 2 * c

    loads = [
        pltpu.make_async_copy(src, dst, lsem.at[n])
        for n, (src, dst) in enumerate(
            [(t_in, tok.at[0, rows(me)]), (s_in, tok.at[1, rows(me)]), (w1t_in, w1t), (w2t_in, w2t),
             (protos_in, protos), (w1s_in, w1s), (w2s_in, w2s)]
        )
    ]
    for load in loads:
        load.start()

    barrier = pltpu.get_barrier_semaphore()

    def greet_proto(k):
        pl.semaphore_signal(barrier, inc=1, device_id=(dp, ring(me + k, npr)), device_id_type=MESH)

    def greet_dp(k):
        pl.semaphore_signal(barrier, inc=1, device_id=(ring(dp + k, ndp), me), device_id_type=MESH)

    loop(1, npr, greet_proto)
    loop(1, ndp, greet_dp)
    loads[0].wait()
    loads[1].wait()
    pl.semaphore_wait(barrier, npr - 1 + ndp - 1)

    def tokens_start(v):
        mine = tok.at[v, rows(me)]
        for k in range(1, nx):
            started(mine, mine, f"tx{v}", dp, proto_of(x + k, y), k)
        for k in range(1, ny):
            started(mine, mine, f"ty{v}", dp, proto_of(x, y + k), k)

    def tokens_forward(v):
        for k in range(1, max(nx, ny)):
            if k < nx:
                block = rows(proto_of(x - k, y))
                arrived(tok.at[v, block], f"tx{v}", k)
                ref = tok.at[v, block, left]
                for m in range(1, ny):
                    started(ref, ref, f"fa{v}", dp, proto_of(x, y + m))
            if k < ny:
                block = rows(proto_of(x, y - k))
                arrived(tok.at[v, block], f"ty{v}", k)
                ref = tok.at[v, block, right]
                for m in range(1, nx):
                    started(ref, ref, f"fb{v}", dp, proto_of(x + m, y))

    diagonal = pl.ds(0, (nx - 1) * (ny - 1) * rb)

    def tokens_wait(v):
        arrived(tok.at[v, diagonal, left], f"fa{v}")
        arrived(tok.at[v, diagonal, right], f"fb{v}")

    def tokens_drain(v):
        gone(tok.at[v, pl.ds(0, (nx - 1) * rb)], f"tx{v}")
        gone(tok.at[v, pl.ds(0, (ny - 1) * rb)], f"ty{v}")
        gone(tok.at[v, diagonal, left], f"fa{v}")
        gone(tok.at[v, diagonal, right], f"fb{v}")

    def head(v):
        step = min(group, 256)

        def chunk(i):
            r = pl.ds(pl.multiple_of(i * step, step), step)
            pre = jnp.dot(tok[v, r, :], w1_of[v][...], preferred_element_type=F32)
            hidden = gelu(pre).astype(BF16)
            if v == 1:
                pre_s[r, :] = pre
                hid_s[r, :] = hidden
            rawp[v, r, :] = jnp.dot(hidden, w2_of[v][...], preferred_element_type=F32)

        loop(0, group // step, chunk, unroll=group // step)

    def raw_send(v):
        def send(k):
            to = ring(me + k, npr)
            started(rawp.at[v, rows(to)], rawr.at[v, k], f"rr{v}", dp, to)

        loop(1, npr, send)

    others = pl.ds(1, npr - 1)

    def raw_finish(v):
        arrived(rawr.at[v, others], f"rr{v}")
        raw = rawp[v, rows(me), :]
        for k in range(1, npr):
            raw = raw + rawr[v, k]
        scale = unit_scale(raw)
        unit_float = raw * scale
        if v == 1:
            own_float[...] = unit_float
            own_scale[...] = scale
        units[v, z, c, rows(me), :] = unit_float.astype(BF16)

    def raw_drain(v):
        gone(rawr.at[v, others], f"rr{v}")

    def band(xx):
        return pl.ds(pl.multiple_of(ring(xx, nx) * (ny * rb), ny * rb), ny * rb)

    def ag_first(v):
        mine = units.at[v, z, c, rows(me)]
        for k in range(1, nz):
            started(mine.at[:, hi], mine.at[:, hi], f"b1{v}", ring(z + k, nz) * 2 + c, me)
        loop(1, npr, lambda k: started(mine.at[:, lo], mine.at[:, lo], f"a1{v}", dp, ring(me + k, npr)))

    def ag_second(v):
        arrived(units.at[v, pl.ds(0, nz - 1), c, rows(me), hi], f"b1{v}")
        col = units.at[v, :, c, rows(me), hi]
        for kx in range(nx):
            for ky in range(ny):
                if kx or ky:
                    started(col, col, f"b2{v}", dp, proto_of(x + kx, y + ky), kx)
        arrived(units.at[v, z, c, pl.ds(0, (npr - 1) * rb), lo], f"a1{v}")
        plane = units.at[v, z, c, :, lo]
        for k in range(1, nz):
            started(plane, plane, f"a2{v}", ring(z + k, nz) * 2 + c, me, k)
        started(plane, plane, f"sa{v}", sib, me)

    def ag_third(v):
        for k in range(1, nz):
            plane = units.at[v, ring(z - k, nz), c, :, lo]
            arrived(plane, f"a2{v}", k)
            started(plane, plane, f"sa{v}", sib, me)
        for k in range(nx):
            piece = units.at[v, :, c, band(x - k), hi]
            if k:
                arrived(piece, f"b2{v}", k)
            else:
                arrived(units.at[v, :, c, pl.ds(0, (ny - 1) * rb), hi], f"b2{v}", k)
            started(piece, piece, f"sb{v}", sib, me)

    def ag_wait(v):
        arrived(units.at[v, :, 1 - c, :, lo], f"sa{v}")
        arrived(units.at[v, :, 1 - c, :, hi], f"sb{v}")

    def ag_drain(v):
        gone(units.at[v, z, c, pl.ds(0, (npr - 1) * rb), lo], f"a1{v}")
        gone(units.at[v, pl.ds(0, nz - 1), c, rows(me), hi], f"b1{v}")
        gone(units.at[v, :, c, pl.ds(0, (npr - 1) * rb), hi], f"b2{v}")
        gone(units.at[v, pl.ds(0, nz - 1), c, :, lo], f"a2{v}")
        gone(units.at[v, :, c, :, lo], f"sa{v}")
        gone(units.at[v, :, c, :, hi], f"sb{v}")

    pb = min(kp, 256)
    nb = kp // pb
    gtiles = group // 128

    def teacher_scores(cc):
        def step(i):
            zz, b = i // nb, i % nb
            r = pl.ds(pl.multiple_of(b * pb, pb), pb)
            s = nt_dot(protos[r, :], units[0, zz, cc])
            e = jnp.exp2(s * (LOG2E / TEACHER_TEMP))
            ex[r, pl.ds(pl.multiple_of((2 * zz + cc) * group, group), group)] = e
            acc = e[:, :128]
            for j in range(1, gtiles):
                acc = acc + e[:, j * 128 : (j + 1) * 128]
            colb[r, :] += acc

        loop(0, nz * nb, step, unroll=2 * nb)

    def first_scales():
        def scale(i):
            r = pl.ds(pl.multiple_of(i * 64, 64), 64)
            total = jnp.sum(colb[r, :], axis=1, keepdims=True)
            colb[r, :] = jnp.broadcast_to(1.0 / (total_protos * total), (64, 128))

        loop(0, kp // 64, scale, unroll=2)

    def student_scores(cc):
        def step(i):
            zz, b = i // nb, i % nb
            r = pl.ds(pl.multiple_of(b * pb, pb), pb)
            lanes = pl.ds(pl.multiple_of((2 * zz + cc) * group, group), group)
            s = nt_dot(protos[r, :], units[1, zz, cc]) * (LOG2E / STUDENT_TEMP)
            lg2[r, lanes] = s
            rows8[:, lanes] += jnp.sum(jnp.exp2(s).reshape(pb // 8, 8, group), axis=0)

        loop(0, nz * nb, step, unroll=2 * nb)

    def row_pass(fresh):
        rows8[...] = jnp.zeros_like(rows8)

        def step(i):
            base = pl.multiple_of(i * 64, 64)
            if fresh:
                accs = [None] * 8
                for j in range(tiles):
                    lanes = slice(j * 128, (j + 1) * 128)
                    w = wb[0:8, lanes]
                    for a in range(8):
                        term = ex[pl.ds(base + 8 * a, 8), lanes] * w
                        accs[a] = term if accs[a] is None else accs[a] + term
                scales = []
                for a in range(8):
                    total = jnp.sum(accs[a], axis=1, keepdims=True)
                    scale = jnp.broadcast_to(1.0 / (total_protos * total), (8, 128))
                    colb[pl.ds(base + 8 * a, 8), :] = scale
                    scales.append(scale)
            else:
                scales = [colb[pl.ds(base + 8 * a, 8), :] for a in range(8)]
            for j in range(tiles):
                lanes = slice(j * 128, (j + 1) * 128)
                terms = [ex[pl.ds(base + 8 * a, 8), lanes] * scales[a] for a in range(8)]
                while len(terms) > 1:
                    terms = [terms[n] + terms[n + 1] for n in range(0, len(terms), 2)]
                rows8[:, lanes] += terms[0]

        loop(0, kp // 64, step, unroll=2)

    def put_rows(t, at):
        for j in range(tiles):
            ps1[t, at * part_rows + j : at * part_rows + j + 1, :] = jnp.sum(
                rows8[:, j * 128 : (j + 1) * 128], axis=0, keepdims=True
            )

    def span(t):
        return pl.ds(0, part_rows * (2 if t == 2 else 1))

    def sum_send(t):
        for k in range(1, ndp):
            started(ps1.at[t, span(t)], psa.at[t, k, span(t)], f"s1{t}", ring(dp + k, ndp), me)

    def sum_middle(t):
        arrived(psa.at[t, pl.ds(1, ndp - 1), span(t)], f"s1{t}")
        total = ps1[t, span(t), :]
        for k in range(1, ndp):
            total = total + psa[t, k, span(t), :]
        psb[t, span(t), :] = total
        for k in range(1, npr):
            started(psb.at[t, span(t)], psbr.at[t, k, span(t)], f"s2{t}", dp, ring(me + k, npr))

    def sum_finish(t):
        arrived(psbr.at[t, others, span(t)], f"s2{t}")
        total = psb[t, span(t), :]
        for k in range(1, npr):
            total = total + psbr[t, k, span(t), :]
        psc[t, span(t), :] = total

    def sum_drain(t):
        gone(psa.at[t, pl.ds(1, ndp - 1), span(t)], f"s1{t}")
        gone(psbr.at[t, others, span(t)], f"s2{t}")

    def spread(t, at, fn, slot):
        for j in range(tiles):
            v = fn(psc[t, at * part_rows + j : at * part_rows + j + 1, :])
            wb[pl.ds(8 * slot, 8), j * 128 : (j + 1) * 128] = jnp.broadcast_to(v, (8, 128))

    def next_weight(v):
        return 1.0 / (crops * v)

    tokens_start(0)
    ps1[...] = jnp.zeros_like(ps1)
    colb[...] = jnp.zeros_like(colb)
    for load in loads[2:]:
        load.wait()
    tokens_forward(0)
    ptr[...] = protos[...].astype(F32).T.astype(BF16)
    tokens_wait(0)
    head(0)
    raw_send(0)
    raw_finish(0)
    ag_first(0)
    tokens_start(1)
    ag_second(0)
    tokens_forward(1)
    ag_third(0)
    teacher_scores(c)
    ag_wait(0)
    teacher_scores(1 - c)
    tokens_wait(1)
    head(1)
    raw_send(1)
    first_scales()
    row_pass(False)
    put_rows(0, 0)
    sum_send(0)
    sum_middle(0)
    raw_finish(1)
    ag_first(1)
    sum_finish(0)
    spread(0, 0, next_weight, 0)
    row_pass(True)
    put_rows(1, 0)
    sum_send(1)
    ag_second(1)
    sum_middle(1)
    ag_third(1)
    rows8[...] = jnp.zeros_like(rows8)
    student_scores(c)
    ag_wait(1)
    student_scores(1 - c)
    put_rows(2, 1)
    sum_finish(1)
    spread(1, 0, next_weight, 0)
    row_pass(True)
    put_rows(2, 0)
    sum_send(2)
    sum_middle(2)
    sum_finish(2)
    spread(2, 0, lambda v: 1.0 / v, 0)
    spread(2, 1, lambda v: jnp.log(v) * LOG2E, 1)

    gp_out[...] = jnp.zeros_like(gp_out)
    losst[...] = jnp.zeros_like(losst)
    share = 1.0 / (crops * STUDENT_TEMP)

    def group_grads(zz, cc):
        lane0 = pl.multiple_of((zz * 2 + cc) * group, group)
        u = units[1, zz, cc]

        def step(b):
            base = pl.multiple_of(b * pb, pb)
            r = pl.ds(base, pb)
            lossa = jnp.zeros((8, 128), F32)
            for j in range(gtiles):
                lanes = pl.ds(pl.multiple_of(lane0 + j * 128, 128), 128)
                inv, norm = wb[0:8, lanes], wb[8:16, lanes]
                for a in range(0, pb, 16):
                    outs = []
                    for h in (0, 8):
                        rr = pl.ds(base + a + h, 8)
                        tgt = ex[rr, lanes] * colb[rr, :] * inv
                        rel = lg2[rr, lanes] - norm
                        lossa = lossa - tgt * rel
                        outs.append((jnp.exp2(rel) - tgt) * share)
                    gt[pl.ds(base + a, 16), j * 128 : (j + 1) * 128] = jnp.concatenate(outs, axis=0).astype(BF16)
            losst[...] += lossa
            gp_out[r, :] += jnp.dot(gt[r, :], u, preferred_element_type=F32)

        loop(0, nb, step, unroll=nb)
        ugt[...] = jnp.dot(ptr[...], gt[...], preferred_element_type=F32)
        return ugt[...].T

    for k in range(nz):
        zz = ring(z + 1 + k, nz)
        sibs[k] = group_grads(zz, 1 - c)
        started(sibs.at[k], sibr.at[k], "g0", sib, me, k)
        mine = group_grads(zz, c)
        arrived(sibr.at[k], "g0", k)
        part[zz] = mine + sibr[k]
        if k < nz - 1:
            started(part.at[zz, :, lo], zrecv.at[k], "gz", zz * 2 + c, me)

        def send(m, zz=zz):
            to = ring(me + m, npr)
            started(part.at[zz, rows(to), hi], precv.at[m, zz], "gp", dp, to)

        loop(1, npr, send)

    arrived(zrecv, "gz")
    total = part[z, :, lo]
    for k in range(nz - 1):
        total = total + zrecv[k]
    a2[...] = total
    loop(1, npr, lambda k: started(a2.at[rows(ring(me + k, npr))], a2r.at[k], "ga", dp, ring(me + k, npr)))

    arrived(precv.at[others], "gp")
    total = part[:, rows(me), hi]
    for k in range(1, npr):
        total = total + precv[k]
    b2[...] = total
    for k in range(1, nz):
        zz = ring(z + k, nz)
        started(b2.at[zz], b2r.at[k], "gb", zz * 2 + c, me)

    losst[...] = losst[...] * (LN2 / crops)
    loop(1, npr, lambda k: started(losst, lossr.at[k], "l1", dp, ring(me + k, npr)))

    arrived(b2r.at[pl.ds(1, nz - 1)], "gb")
    grad_hi = b2[z]
    for k in range(1, nz):
        grad_hi = grad_hi + b2r[k]
    arrived(a2r.at[others], "ga")
    grad_lo = a2[rows(me), :]
    for k in range(1, npr):
        grad_lo = grad_lo + a2r[k]

    unit_grad = jnp.concatenate([grad_lo, grad_hi], axis=1)
    own = own_float[...]
    along = jnp.sum(own * unit_grad, axis=1, keepdims=True)
    rg[rows(me), :] = ((unit_grad - own * along) * own_scale[...]).astype(BF16)
    loop(1, npr, lambda k: started(rg.at[rows(me)], rg.at[rows(me)], "r1", dp, ring(me + k, npr)))

    arrived(lossr.at[others], "l1")
    total = losst[...]
    for k in range(1, npr):
        total = total + lossr[k]
    lossd[...] = total
    loop(1, ndp, lambda k: started(lossd, lossdr.at[k], "l2", ring(dp + k, ndp), me))
    pre_s[...] = gelu_slope(pre_s[...])

    arrived(rg.at[pl.ds(0, (npr - 1) * rb)], "r1")
    raw_grad = rg[...]
    pre_grad = (nt_dot(raw_grad, w2s[...]) * pre_s[...]).astype(BF16)
    w2g = tn_dot(hid_s[...], raw_grad)
    gw[pl.ds(width, hb), :] = w2g[:, :hb]
    gw[pl.ds(width + hb, hb), :] = w2g[:, hb:]
    wchunk = min(width, 256)
    for i in range(width // wchunk):
        sl = slice(i * wchunk, (i + 1) * wchunk)
        gw[sl, :] = tn_dot(tok[1, :, sl], pre_grad)

    whole = gw.shape[0]
    halfw, piece = whole // 2, whole // ndp

    def half_of(cc):
        return pl.ds(pl.multiple_of(cc * halfw, 8), halfw)

    def piece_of(zz):
        return pl.ds(pl.multiple_of(c * halfw + zz * piece, 8), piece)

    started(gw.at[half_of(1 - c)], gwr, "w0", sib, me)
    arrived(gwr, "w0")
    gw[half_of(c), :] += gwr[...]
    for k in range(1, nz):
        zz = ring(z + k, nz)
        started(gw.at[piece_of(zz)], gwz.at[k], "w1", zz * 2 + c, me)
    total = gw[piece_of(z), :]
    arrived(gwz.at[pl.ds(1, nz - 1)], "w1")
    for k in range(1, nz):
        total = total + gwz[k]
    fw[piece_of(z), :] = total
    for k in range(1, nz):
        started(fw.at[piece_of(z)], fw.at[piece_of(z)], "w2", ring(z + k, nz) * 2 + c, me)
    arrived(gwz.at[pl.ds(1, nz - 1)], "w2")
    started(fw.at[half_of(c)], fw.at[half_of(c)], "w3", sib, me)

    arrived(lossdr.at[pl.ds(1, ndp - 1)], "l2")
    loss = lossd[...]
    for k in range(1, ndp):
        loss = loss + lossdr[k]
    loss_out[...] = jnp.sum(jnp.sum(loss, axis=0, keepdims=True), axis=1, keepdims=True)

    for v in (0, 1):
        tokens_drain(v)
        raw_drain(v)
        ag_drain(v)
    for t in range(3):
        sum_drain(t)
    gone(sibs, "g0")
    gone(zrecv, "gz")
    gone(precv.at[others], "gp")
    gone(a2r.at[others], "ga")
    gone(b2r.at[pl.ds(1, nz - 1)], "gb")
    gone(lossr.at[others], "l1")
    gone(lossdr.at[pl.ds(1, ndp - 1)], "l2")
    gone(rg.at[pl.ds(0, (npr - 1) * rb)], "r1")
    gone(gwr, "w0")
    gone(gwz.at[pl.ds(1, nz - 1)], "w1")
    gone(gwz.at[pl.ds(1, nz - 1)], "w2")

    arrived(fw.at[half_of(1 - c)], "w3")
    gw1_out[...] = fw[:width, :]
    gw2_out[:, :hb] = fw[width : width + hb, :]
    gw2_out[:, hb:] = fw[width + hb :, :]
    gone(gwr, "w3")


def step(dims, s_in, t_in, w1s, w2s, w1t, w2t, protos):
    nz, nx, ny = dims["nz"], dims["nx"], dims["ny"]
    ndp, npr = 2 * nz, nx * ny
    rb, width = s_in.shape
    hb, cols = w2s.shape
    kp = protos.shape[0]
    group = rb * npr
    crops = group * ndp
    half = cols // 2
    dims = dict(dims, rb=rb, q=group // 128)

    plan, n_send, n_recv = {}, 0, 0
    phases = [(f"{name}{v}", n) for v in (0, 1) for name, n in dict(
        tx=nx, ty=ny, fa=1, fb=1, rr=1, a1=1, b1=1, b2=nx, a2=nz, sa=1, sb=1).items()]
    phases += [(f"{name}{t}", 1) for t in range(3) for name in ("s1", "s2")]
    phases += [("g0", nz)] + [(n, 1) for n in ("gz", "gp", "ga", "gb", "l1", "l2", "r1", "w0", "w1", "w2", "w3")]
    for name, n in phases:
        plan[name] = (n_send, n_recv)
        n_send, n_recv = n_send + 1, n_recv + n
    part_rows = max(8, crops // 128)

    wrows = width + 2 * hb
    V = pltpu.VMEM
    scratch = [
        V((width, hb), BF16),
        V((hb, cols), BF16),
        V((width, hb), BF16),
        V((hb, cols), BF16),
        V((kp, cols), BF16),
        V((2, group, width), BF16),
        V((group, hb), F32),
        V((group, hb), BF16),
        V((2, group, cols), F32),
        V((2, npr, rb, cols), F32),
        V((2, nz, 2, group, cols), BF16),
        V((rb, cols), F32),
        V((rb, 1), F32),
        V((kp, crops), F32),
        V((kp, crops), F32),
        V((kp, 128), F32),
        V((16, crops), F32),
        V((8, crops), F32),
        V((3, 2 * part_rows, 128), F32),
        V((3, ndp, 2 * part_rows, 128), F32),
        V((3, 2 * part_rows, 128), F32),
        V((3, npr, 2 * part_rows, 128), F32),
        V((3, 2 * part_rows, 128), F32),
        V((kp, group), BF16),
        V((cols, kp), BF16),
        V((cols, group), F32),
        V((nz, group, cols), F32),
        V((nz, group, cols), F32),
        V((nz, group, cols), F32),
        V((nz - 1, group, half), F32),
        V((npr, nz, rb, half), F32),
        V((group, half), F32),
        V((npr, rb, half), F32),
        V((nz, rb, half), F32),
        V((nz, rb, half), F32),
        V((8, 128), F32),
        V((npr, 8, 128), F32),
        V((8, 128), F32),
        V((ndp, 8, 128), F32),
        V((group, cols), BF16),
        V((wrows, hb), F32),
        V((wrows // 2, hb), F32),
        V((nz, wrows // ndp, hb), F32),
        V((wrows, hb), F32),
        pltpu.SemaphoreType.DMA((n_send,)),
        pltpu.SemaphoreType.DMA((n_recv,)),
        pltpu.SemaphoreType.DMA((7,)),
    ]
    vmem = pl.BlockSpec(memory_space=pltpu.VMEM)
    gp, gw1, gw2, loss = pl.pallas_call(
        functools.partial(kernel, dims, plan),
        out_shape=(
            jax.ShapeDtypeStruct((kp, cols), F32),
            jax.ShapeDtypeStruct((width, hb), F32),
            jax.ShapeDtypeStruct((hb, cols), F32),
            jax.ShapeDtypeStruct((1, 1), F32),
        ),
        in_specs=[pl.BlockSpec(memory_space=pl.ANY)] * 7,
        out_specs=(vmem,) * 4,
        scratch_shapes=scratch,
        compiler_params=pltpu.CompilerParams(
            collective_id=0, has_side_effects=True, vmem_limit_bytes=63 * 1024 * 1024
        ),
        cost_estimate=pl.CostEstimate(
            flops=8 * kp * crops * cols, bytes_accessed=4 * kp * cols * 4, transcendentals=2 * kp * crops
        ),
    )(s_in, t_in, w1s, w2s, w1t, w2t, protos)
    return gp, gw1, gw2, loss[0, 0]


def solution(mesh):
    ndp, npr = mesh.shape["dp"], mesh.shape["proto"]
    side = math.isqrt(npr)
    dims = dict(nz=ndp // 2, nx=side, ny=npr // side)
    both = P(("dp", "proto"), None)
    return jax.shard_map(
        functools.partial(step, dims),
        mesh=mesh,
        in_specs=(both, both, P(None, "proto"), P("proto", None), P(None, "proto"), P("proto", None), both),
        out_specs=(both, P(None, "proto"), P("proto", None), P()),
        check_vma=False,
    )
```

time: 195 us -> 155 us (0.79)
  Pallas kernels: 188 us -> 149 us
    pallas_call x1, Pallas kernels: 188 us -> 149 us  [step(): pl.pallas_call(functools.partial(kernel, dims, plan), out_shape=(jax.Shap...]
where the time goes in v2:
time: 155 us
  Pallas kernels  149 us (96%)
  local copies, waits for them, and re-layouts  4.02 us (3%)
  between operations  2.42 us (2%)
    pallas_call x1, Pallas kernels, step(): pl.pallas_call(functools.partial(kernel, dims, plan), out_shape=(jax.Shap...  149 us
    unnamed x7, local copies, waits for them, and re-layouts  4.02 us

profile of v2, /device:TPU:1, one launch (start us, length us, event | category | flops | bytes accessed | tf_op | source)
XLA Modules:
  0.0 155.2 jit_solution(17618906418937317583)
XLA Ops:
  0.6 148.8 %shard_map.102 = (f32[1024,256]{1,0:T(8,128)}, f32[1536,128]{1,0:T(8,128)}, f32[128,256]{1,0:T(8,128)}, f32[1,1]{1,0:T(1,128)}) custom-call(bf16[32,1536]{1,0:T(8,128)(2,1)} %s_in.1, bf16[32,1536]{1,0:T(8,128)(2,1)} %t_in.1, bf16[1536,128]{1,0:T(8,128)(2,1)} %w1s_in.1, bf16[128,256]{1,0:T(8,128)(2,1)} %w2s_in.1, bf16[1536,128]{1,0:T(8,128)(2,1)} %w1t_in.1, ...), custom_call_target="tpu_custom_call" | custom-call | flops 8589934592 | bytes 4194304 | tf_op jit(solution)/shard_map/pallas_call | solution.py:629
  149.4 0.0 copy-start
  149.4 2.3 %copy.15 = f32[1024,256]{1,0:T(8,128)} copy(f32[1024,256]{1,0:T(8,128)} %get-tuple-element.16) | data formatting | bytes 2097152
  151.7 0.0 copy-done
  151.7 0.0 copy-start.1
  151.7 0.9 copy.16
  152.6 0.1 copy-done.1
  152.8 0.7 copy.17
Async XLA Ops:
  149.4 2.3 %copy-start = (f32[1536,128]{1,0:T(8,128)S(1)}, f32[1536,128]{1,0:T(8,128)}, u32[]{:S(2)}) copy-start(f32[1536,128]{1,0:T(8,128)} %get-tuple-element.17) | copy-start | bytes 2359300
  151.7 1.0 copy-start.1

commit v3 on v2

--- a/solution.py
+++ b/solution.py
@@ -51,8 +51,9 @@
     tiles = crops // 128
     part_rows = max(8, tiles)
     half = cols // 2
+    hr = rb // 2
     (w1s, w2s, w1t, w2t, protos, tok, pre_s, hid_s, rawp, rawr, units, own_float, own_scale, ex, lg2, colb, wb, rows8,
-     ps1, psa, psb, psbr, psc, gt, ptr, ugt, sibs, sibr, part, zrecv, precv, a2, a2r, b2, b2r, losst, lossr, lossd,
+     ps1, psa, psb, psbr, psc, gt, ptr, ugt, sibs, sibr, part, zrecv, precv, ohr, a2, a2r, b2, b2r, losst, lossr, lossd,
      lossdr, rg, gw, gwr, gwz, fw, ssem, rsem, lsem) = scratch
 
     dp, me = lax.axis_index("dp"), lax.axis_index("proto")
@@ -84,6 +85,9 @@
 
     def rows(p):
         return pl.ds(pl.multiple_of(p * rb, rb), rb)
+
+    def hrows(p):
+        return pl.ds(pl.multiple_of(p * hr, hr), hr)
 
     def ring(value, n):
         return lax.rem(value + n, n)
@@ -185,57 +189,74 @@
         if v == 1:
             own_float[...] = unit_float
             own_scale[...] = scale
-        units[v, z, c, rows(me), :] = unit_float.astype(BF16)
+        units[v, z, c, :, hrows(me), :] = unit_float.astype(BF16).reshape(2, hr, cols)
 
     def raw_drain(v):
         gone(rawr.at[v, others], f"rr{v}")
 
     def band(xx):
-        return pl.ds(pl.multiple_of(ring(xx, nx) * (ny * rb), ny * rb), ny * rb)
+        return pl.ds(pl.multiple_of(ring(xx, nx) * (ny * hr), ny * hr), ny * hr)
 
     def ag_first(v):
-        mine = units.at[v, z, c, rows(me)]
+        mine = units.at[v, z, c, 1, hrows(me)]
         for k in range(1, nz):
             started(mine.at[:, hi], mine.at[:, hi], f"b1{v}", ring(z + k, nz) * 2 + c, me)
         loop(1, npr, lambda k: started(mine.at[:, lo], mine.at[:, lo], f"a1{v}", dp, ring(me + k, npr)))
+        direct = units.at[v, z, c, 0, hrows(me)]
+        for kz in list(range(1, nz)) + [0]:
+
+            def send(k, kz=kz):
+                started(direct, direct, f"d1{v}", ring(z + kz, nz) * 2 + c, ring(me + k, npr), kz)
+
+            loop(0 if kz else 1, npr, send)
 
     def ag_second(v):
-        arrived(units.at[v, pl.ds(0, nz - 1), c, rows(me), hi], f"b1{v}")
-        col = units.at[v, :, c, rows(me), hi]
+        arrived(units.at[v, pl.ds(0, nz - 1), c, 1, hrows(me), hi], f"b1{v}")
+        col = units.at[v, :, c, 1, hrows(me), hi]
         for kx in range(nx):
             for ky in range(ny):
                 if kx or ky:
                     started(col, col, f"b2{v}", dp, proto_of(x + kx, y + ky), kx)
-        arrived(units.at[v, z, c, pl.ds(0, (npr - 1) * rb), lo], f"a1{v}")
-        plane = units.at[v, z, c, :, lo]
+        arrived(units.at[v, z, c, 1, pl.ds(0, (npr - 1) * hr), lo], f"a1{v}")
+        plane = units.at[v, z, c, 1, :, lo]
         for k in range(1, nz):
             started(plane, plane, f"a2{v}", ring(z + k, nz) * 2 + c, me, k)
         started(plane, plane, f"sa{v}", sib, me)
 
     def ag_third(v):
+        for k in range(nz):
+            plane = units.at[v, ring(z - k, nz), c, 0]
+            if k:
+                arrived(plane, f"d1{v}", k)
+            else:
+                arrived(units.at[v, z, c, 0, pl.ds(0, (npr - 1) * hr)], f"d1{v}", k)
+            started(plane, plane, f"sd{v}", sib, me)
         for k in range(1, nz):
-            plane = units.at[v, ring(z - k, nz), c, :, lo]
+            plane = units.at[v, ring(z - k, nz), c, 1, :, lo]
             arrived(plane, f"a2{v}", k)
             started(plane, plane, f"sa{v}", sib, me)
         for k in range(nx):
-            piece = units.at[v, :, c, band(x - k), hi]
+            piece = units.at[v, :, c, 1, band(x - k), hi]
             if k:
                 arrived(piece, f"b2{v}", k)
             else:
-                arrived(units.at[v, :, c, pl.ds(0, (ny - 1) * rb), hi], f"b2{v}", k)
+                arrived(units.at[v, :, c, 1, pl.ds(0, (ny - 1) * hr), hi], f"b2{v}", k)
             started(piece, piece, f"sb{v}", sib, me)
 
     def ag_wait(v):
-        arrived(units.at[v, :, 1 - c, :, lo], f"sa{v}")
-        arrived(units.at[v, :, 1 - c, :, hi], f"sb{v}")
+        arrived(units.at[v, :, 1 - c, 0], f"sd{v}")
+        arrived(units.at[v, :, 1 - c, 1, :, lo], f"sa{v}")
+        arrived(units.at[v, :, 1 - c, 1, :, hi], f"sb{v}")
 
     def ag_drain(v):
-        gone(units.at[v, z, c, pl.ds(0, (npr - 1) * rb), lo], f"a1{v}")
-        gone(units.at[v, pl.ds(0, nz - 1), c, rows(me), hi], f"b1{v}")
-        gone(units.at[v, :, c, pl.ds(0, (npr - 1) * rb), hi], f"b2{v}")
-        gone(units.at[v, pl.ds(0, nz - 1), c, :, lo], f"a2{v}")
-        gone(units.at[v, :, c, :, lo], f"sa{v}")
-        gone(units.at[v, :, c, :, hi], f"sb{v}")
+        gone(protos.at[pl.ds(0, (nz * npr - 1) * hr)], f"d1{v}")
+        gone(units.at[v, :, c, 0], f"sd{v}")
+        gone(units.at[v, z, c, 1, pl.ds(0, (npr - 1) * hr), lo], f"a1{v}")
+        gone(units.at[v, pl.ds(0, nz - 1), c, 1, hrows(me), hi], f"b1{v}")
+        gone(units.at[v, :, c, 1, pl.ds(0, (npr - 1) * hr), hi], f"b2{v}")
+        gone(units.at[v, pl.ds(0, nz - 1), c, 1, :, lo], f"a2{v}")
+        gone(units.at[v, :, c, 1, :, lo], f"sa{v}")
+        gone(units.at[v, :, c, 1, :, hi], f"sb{v}")
 
     pb = min(kp, 256)
     nb = kp // pb
@@ -245,7 +266,7 @@
         def step(i):
             zz, b = i // nb, i % nb
             r = pl.ds(pl.multiple_of(b * pb, pb), pb)
-            s = nt_dot(protos[r, :], units[0, zz, cc])
+            s = nt_dot(protos[r, :], units[0, zz, cc].reshape(group, cols))
             e = jnp.exp2(s * (LOG2E / TEACHER_TEMP))
             ex[r, pl.ds(pl.multiple_of((2 * zz + cc) * group, group), group)] = e
             acc = e[:, :128]
@@ -268,7 +289,7 @@
             zz, b = i // nb, i % nb
             r = pl.ds(pl.multiple_of(b * pb, pb), pb)
             lanes = pl.ds(pl.multiple_of((2 * zz + cc) * group, group), group)
-            s = nt_dot(protos[r, :], units[1, zz, cc]) * (LOG2E / STUDENT_TEMP)
+            s = nt_dot(protos[r, :], units[1, zz, cc].reshape(group, cols)) * (LOG2E / STUDENT_TEMP)
             lg2[r, lanes] = s
             rows8[:, lanes] += jnp.sum(jnp.exp2(s).reshape(pb // 8, 8, group), axis=0)
 
@@ -403,7 +424,7 @@
 
     def group_grads(zz, cc):
         lane0 = pl.multiple_of((zz * 2 + cc) * group, group)
-        u = units[1, zz, cc]
+        u = units[1, zz, cc].reshape(group, cols)
 
         def step(b):
             base = pl.multiple_of(b * pb, pb)
@@ -426,53 +447,66 @@
 
         loop(0, nb, step, unroll=nb)
         ugt[...] = jnp.dot(ptr[...], gt[...], preferred_element_type=F32)
-        return ugt[...].T
-
-    for k in range(nz):
-        zz = ring(z + 1 + k, nz)
-        sibs[k] = group_grads(zz, 1 - c)
-        started(sibs.at[k], sibr.at[k], "g0", sib, me, k)
+        return ugt[...].T.reshape(2, group // 2, cols)
+
+    planes = sorted(range(1, nz), key=lambda k: -min(k, nz - k)) + [0]
+    for n, k in enumerate(planes):
+        zz = ring(z + k, nz)
+        sibs[n] = group_grads(zz, 1 - c)
+        started(sibs.at[n], sibr.at[n], "g0", sib, me, n)
         mine = group_grads(zz, c)
-        arrived(sibr.at[k], "g0", k)
-        part[zz] = mine + sibr[k]
-        if k < nz - 1:
-            started(part.at[zz, :, lo], zrecv.at[k], "gz", zz * 2 + c, me)
-
-        def send(m, zz=zz):
+        arrived(sibr.at[n], "g0", n)
+        part[k] = mine + sibr[n]
+        if k:
+            for h in range(2):
+                started(part.at[k, h, :, lo], zrecv.at[h, k - 1], "gz", zz * 2 + c, me, h)
+
+        def send(m, k=k):
             to = ring(me + m, npr)
-            started(part.at[zz, rows(to), hi], precv.at[m, zz], "gp", dp, to)
+            if k:
+                started(part.at[k, :, hrows(to), hi], precv.at[m, k - 1], "gp", dp, to)
+            else:
+                started(part.at[k, :, hrows(to), hi], ohr.at[m], "go", dp, to)
 
         loop(1, npr, send)
 
-    arrived(zrecv, "gz")
-    total = part[z, :, lo]
-    for k in range(nz - 1):
-        total = total + zrecv[k]
-    a2[...] = total
-    loop(1, npr, lambda k: started(a2.at[rows(ring(me + k, npr))], a2r.at[k], "ga", dp, ring(me + k, npr)))
-
-    arrived(precv.at[others], "gp")
-    total = part[:, rows(me), hi]
-    for k in range(1, npr):
-        total = total + precv[k]
-    b2[...] = total
-    for k in range(1, nz):
-        zz = ring(z + k, nz)
-        started(b2.at[zz], b2r.at[k], "gb", zz * 2 + c, me)
+    for h in range(2):
+        arrived(zrecv.at[h], "gz", h)
+        total = part[0, h, :, lo]
+        for k in range(nz - 1):
+            total = total + zrecv[h, k]
+        a2[h] = total
+
+        def send(k, h=h):
+            to = ring(me + k, npr)
+            started(a2.at[h, hrows(to)], a2r.at[k, h], "ga", dp, to)
+
+        loop(1, npr, send)
+        if h == 0:
+            arrived(precv.at[others], "gp")
+            total = part[pl.ds(1, nz - 1), :, hrows(me), hi]
+            for k in range(1, npr):
+                total = total + precv[k]
+            b2[...] = total
+            for k in range(1, nz):
+                started(b2.at[k - 1], b2r.at[k - 1], "gb", ring(z + k, nz) * 2 + c, me)
 
     losst[...] = losst[...] * (LN2 / crops)
     loop(1, npr, lambda k: started(losst, lossr.at[k], "l1", dp, ring(me + k, npr)))
 
-    arrived(b2r.at[pl.ds(1, nz - 1)], "gb")
-    grad_hi = b2[z]
-    for k in range(1, nz):
+    arrived(ohr.at[others], "go")
+    grad_hi = part[0, :, hrows(me), hi]
+    for k in range(1, npr):
+        grad_hi = grad_hi + ohr[k]
+    arrived(b2r, "gb")
+    for k in range(nz - 1):
         grad_hi = grad_hi + b2r[k]
     arrived(a2r.at[others], "ga")
-    grad_lo = a2[rows(me), :]
+    grad_lo = a2[:, hrows(me), :]
     for k in range(1, npr):
         grad_lo = grad_lo + a2r[k]
 
-    unit_grad = jnp.concatenate([grad_lo, grad_hi], axis=1)
+    unit_grad = jnp.concatenate([grad_lo.reshape(rb, half), grad_hi.reshape(rb, half)], axis=1)
     own = own_float[...]
     along = jnp.sum(own * unit_grad, axis=1, keepdims=True)
     rg[rows(me), :] = ((unit_grad - own * along) * own_scale[...]).astype(BF16)
@@ -489,38 +523,50 @@
     arrived(rg.at[pl.ds(0, (npr - 1) * rb)], "r1")
     raw_grad = rg[...]
     pre_grad = (nt_dot(raw_grad, w2s[...]) * pre_s[...]).astype(BF16)
-    w2g = tn_dot(hid_s[...], raw_grad)
-    gw[pl.ds(width, hb), :] = w2g[:, :hb]
-    gw[pl.ds(width + hb, hb), :] = w2g[:, hb:]
+    whole = gw.shape[0]
+    parts = 2
+    share_rows, piece = whole // (2 * parts), whole // (ndp * parts)
+
+    def half_of(n, cc):
+        return pl.ds(pl.multiple_of((2 * n + cc) * share_rows, 8), share_rows)
+
+    def piece_of(n, zz):
+        return pl.ds(pl.multiple_of((2 * n + c) * share_rows + zz * piece, 8), piece)
+
     wchunk = min(width, 256)
-    for i in range(width // wchunk):
-        sl = slice(i * wchunk, (i + 1) * wchunk)
-        gw[sl, :] = tn_dot(tok[1, :, sl], pre_grad)
-
-    whole = gw.shape[0]
-    halfw, piece = whole // 2, whole // ndp
-
-    def half_of(cc):
-        return pl.ds(pl.multiple_of(cc * halfw, 8), halfw)
-
-    def piece_of(zz):
-        return pl.ds(pl.multiple_of(c * halfw + zz * piece, 8), piece)
-
-    started(gw.at[half_of(1 - c)], gwr, "w0", sib, me)
-    arrived(gwr, "w0")
-    gw[half_of(c), :] += gwr[...]
-    for k in range(1, nz):
-        zz = ring(z + k, nz)
-        started(gw.at[piece_of(zz)], gwz.at[k], "w1", zz * 2 + c, me)
-    total = gw[piece_of(z), :]
-    arrived(gwz.at[pl.ds(1, nz - 1)], "w1")
-    for k in range(1, nz):
-        total = total + gwz[k]
-    fw[piece_of(z), :] = total
-    for k in range(1, nz):
-        started(fw.at[piece_of(z)], fw.at[piece_of(z)], "w2", ring(z + k, nz) * 2 + c, me)
-    arrived(gwz.at[pl.ds(1, nz - 1)], "w2")
-    started(fw.at[half_of(c)], fw.at[half_of(c)], "w3", sib, me)
+    sent = 0
+    for i in range(width // wchunk + 1):
+        if i < width // wchunk:
+            sl = slice(i * wchunk, (i + 1) * wchunk)
+            gw[sl, :] = tn_dot(tok[1, :, sl], pre_grad)
+            done = (i + 1) * wchunk
+        else:
+            w2g = tn_dot(hid_s[...], raw_grad)
+            gw[pl.ds(width, hb), :] = w2g[:, :hb]
+            gw[pl.ds(width + hb, hb), :] = w2g[:, hb:]
+            done = whole
+        while sent < parts and done >= 2 * (sent + 1) * share_rows:
+            started(gw.at[half_of(sent, 1 - c)], gwr.at[sent], "w0", sib, me, sent)
+            sent += 1
+
+    zpeers = pl.ds(1, nz - 1)
+    for n in range(parts):
+        arrived(gwr.at[n], "w0", n)
+        gw[half_of(n, c), :] += gwr[n]
+        for k in range(1, nz):
+            zz = ring(z + k, nz)
+            started(gw.at[piece_of(n, zz)], gwz.at[n, k], "w1", zz * 2 + c, me, n)
+    for n in range(parts):
+        total = gw[piece_of(n, z), :]
+        arrived(gwz.at[n, zpeers], "w1", n)
+        for k in range(1, nz):
+            total = total + gwz[n, k]
+        fw[piece_of(n, z), :] = total
+        for k in range(1, nz):
+            started(fw.at[piece_of(n, z)], fw.at[piece_of(n, z)], "w2", ring(z + k, nz) * 2 + c, me, n)
+    for n in range(parts):
+        arrived(gwz.at[n, zpeers], "w2", n)
+        started(fw.at[half_of(n, c)], fw.at[half_of(n, c)], "w3", sib, me)
 
     arrived(lossdr.at[pl.ds(1, ndp - 1)], "l2")
     loss = lossd[...]
@@ -536,17 +582,18 @@
         sum_drain(t)
     gone(sibs, "g0")
     gone(zrecv, "gz")
+    gone(ohr.at[others], "go")
     gone(precv.at[others], "gp")
     gone(a2r.at[others], "ga")
-    gone(b2r.at[pl.ds(1, nz - 1)], "gb")
+    gone(b2r, "gb")
     gone(lossr.at[others], "l1")
     gone(lossdr.at[pl.ds(1, ndp - 1)], "l2")
     gone(rg.at[pl.ds(0, (npr - 1) * rb)], "r1")
     gone(gwr, "w0")
-    gone(gwz.at[pl.ds(1, nz - 1)], "w1")
-    gone(gwz.at[pl.ds(1, nz - 1)], "w2")
-
-    arrived(fw.at[half_of(1 - c)], "w3")
+    gone(gwz.at[:, zpeers], "w1")
+    gone(gwz.at[:, zpeers], "w2")
+
+    arrived(gwr, "w3")
     gw1_out[...] = fw[:width, :]
     gw2_out[:, :hb] = fw[width : width + hb, :]
     gw2_out[:, hb:] = fw[width + hb :, :]
@@ -566,9 +613,10 @@
 
     plan, n_send, n_recv = {}, 0, 0
     phases = [(f"{name}{v}", n) for v in (0, 1) for name, n in dict(
-        tx=nx, ty=ny, fa=1, fb=1, rr=1, a1=1, b1=1, b2=nx, a2=nz, sa=1, sb=1).items()]
+        tx=nx, ty=ny, fa=1, fb=1, rr=1, a1=1, b1=1, b2=nx, a2=nz, d1=nz, sa=1, sb=1, sd=1).items()]
     phases += [(f"{name}{t}", 1) for t in range(3) for name in ("s1", "s2")]
-    phases += [("g0", nz)] + [(n, 1) for n in ("gz", "gp", "ga", "gb", "l1", "l2", "r1", "w0", "w1", "w2", "w3")]
+    phases += [("g0", nz), ("gz", 2), ("w0", 2), ("w1", 2), ("w2", 2)]
+    phases += [(n, 1) for n in ("gp", "go", "ga", "gb", "l1", "l2", "r1", "w3")]
     for name, n in phases:
         plan[name] = (n_send, n_recv)
         n_send, n_recv = n_send + 1, n_recv + n
@@ -587,7 +635,7 @@
         V((group, hb), BF16),
         V((2, group, cols), F32),
         V((2, npr, rb, cols), F32),
-        V((2, nz, 2, group, cols), BF16),
+        V((2, nz, 2, 2, group // 2, cols), BF16),
         V((rb, cols), F32),
         V((rb, 1), F32),
         V((kp, crops), F32),
@@ -603,23 +651,24 @@
         V((kp, group), BF16),
         V((cols, kp), BF16),
         V((cols, group), F32),
-        V((nz, group, cols), F32),
-        V((nz, group, cols), F32),
-        V((nz, group, cols), F32),
-        V((nz - 1, group, half), F32),
-        V((npr, nz, rb, half), F32),
-        V((group, half), F32),
-        V((npr, rb, half), F32),
-        V((nz, rb, half), F32),
-        V((nz, rb, half), F32),
+        V((nz, 2, group // 2, cols), F32),
+        V((nz, 2, group // 2, cols), F32),
+        V((nz, 2, group // 2, cols), F32),
+        V((2, nz - 1, group // 2, half), F32),
+        V((npr, nz - 1, 2, rb // 2, half), F32),
+        V((npr, 2, rb // 2, half), F32),
+        V((2, group // 2, half), F32),
+        V((npr, 2, rb // 2, half), F32),
+        V((nz - 1, 2, rb // 2, half), F32),
+        V((nz - 1, 2, rb // 2, half), F32),
         V((8, 128), F32),
         V((npr, 8, 128), F32),
         V((8, 128), F32),
         V((ndp, 8, 128), F32),
         V((group, cols), BF16),
         V((wrows, hb), F32),
-        V((wrows // 2, hb), F32),
-        V((nz, wrows // ndp, hb), F32),
+        V((2, wrows // 4, hb), F32),
+        V((2, nz, wrows // (2 * ndp), hb), F32),
         V((wrows, hb), F32),
         pltpu.SemaphoreType.DMA((n_send,)),
         pltpu.SemaphoreType.DMA((n_recv,)),
@@ -629,16 +678,16 @@
     gp, gw1, gw2, loss = pl.pallas_call(
         functools.partial(kernel, dims, plan),
         out_shape=(
-            jax.ShapeDtypeStruct((kp, cols), F32),
-            jax.ShapeDtypeStruct((width, hb), F32),
-            jax.ShapeDtypeStruct((hb, cols), F32),
+            pltpu.VMEM((kp, cols), F32),
+            pltpu.VMEM((width, hb), F32),
+            pltpu.VMEM((hb, cols), F32),
             jax.ShapeDtypeStruct((1, 1), F32),
         ),
         in_specs=[pl.BlockSpec(memory_space=pl.ANY)] * 7,
         out_specs=(vmem,) * 4,
         scratch_shapes=scratch,
         compiler_params=pltpu.CompilerParams(
-            collective_id=0, has_side_effects=True, vmem_limit_bytes=63 * 1024 * 1024
+            collective_id=0, has_side_effects=True, vmem_limit_bytes=61 * 1024 * 1024
         ),
         cost_estimate=pl.CostEstimate(
             flops=8 * kp * crops * cols, bytes_accessed=4 * kp * cols * 4, transcendentals=2 * kp * crops

time: 155 us -> 149 us (0.961)
  Pallas kernels: 149 us -> 144 us
    pallas_call x1, Pallas kernels: 149 us -> 144 us  [step(): pl.pallas_call(functools.partial(kernel, dims, plan), out_shape=(pltpu.VM...]
    unnamed x7 -> x3, local copies, waits for them, and re-layouts: 4.02 us -> 2.51 us
where the time goes in v3:
time: 149 us
  Pallas kernels  144 us (97%)
  local copies, waits for them, and re-layouts  2.51 us (2%)
  between operations  2.33 us (2%)
    pallas_call x1, Pallas kernels, step(): pl.pallas_call(functools.partial(kernel, dims, plan), out_shape=(pltpu.VM...  144 us

profile of v3, /device:TPU:1, one launch (start us, length us, event | category | flops | bytes accessed | tf_op | source)
XLA Modules:
  0.0 149.2 jit_solution(13163872808801472218)
XLA Ops:
  0.6 144.4 %shard_map.102 = (f32[1024,256]{1,0:T(8,128)S(1)}, f32[1536,128]{1,0:T(8,128)S(1)}, f32[128,256]{1,0:T(8,128)S(1)}, f32[1,1]{1,0:T(1,128)}) custom-call(bf16[32,1536]{1,0:T(8,128)(2,1)} %s_in.1, bf16[32,1536]{1,0:T(8,128)(2,1)} %t_in.1, bf16[1536,128]{1,0:T(8,128)(2,1)} %w1s_in.1, bf16[128,256]{1,0:T(8,128)(2,1)} %w2s_in.1, bf16[1536,128]{1,0:T(8,128)(2,1)} %w1t_in.1, ...), custom_call_target="tpu_custom_call" | custom-call | flops 8589934592 | bytes 4194304 | tf_op jit(solution)/shard_map/pallas_call | solution.py:678
  145.0 1.0 copy.15
  146.0 0.7 copy.17
  146.7 0.9 copy.16

commit v4 on v3

--- a/solution.py
+++ b/solution.py
@@ -52,7 +52,7 @@
     part_rows = max(8, tiles)
     half = cols // 2
     hr = rb // 2
-    (w1s, w2s, w1t, w2t, protos, tok, pre_s, hid_s, rawp, rawr, units, own_float, own_scale, ex, lg2, colb, wb, rows8,
+    (w1s, w2s, w1g, w2g, protos, tok, pre_s, hid_s, rawp, rawr, units, own_float, own_scale, ex, lg2, colb, wb, rows8,
      ps1, psa, psb, psbr, psc, gt, ptr, ugt, sibs, sibr, part, zrecv, precv, ohr, a2, a2r, b2, b2r, losst, lossr, lossd,
      lossdr, rg, gw, gwr, gwz, fw, ssem, rsem, lsem) = scratch
 
@@ -60,8 +60,8 @@
     z, c = dp // 2, dp % 2
     x, y = me // ny, me % ny
 
-    def started(src, dst, name, to_dp, to_proto, nth=0):
-        s, r = plan[name]
+    def started(src, dst, name, to_dp, to_proto, nth=0, send_as=None):
+        s, r = plan[send_as or name][0], plan[name][1]
         pltpu.make_async_remote_copy(
             src_ref=src, dst_ref=dst, send_sem=ssem.at[s], recv_sem=rsem.at[r + nth],
             device_id=(to_dp, to_proto), device_id_type=MESH,
@@ -92,21 +92,33 @@
     def ring(value, n):
         return lax.rem(value + n, n)
 
-    inputs = (t_in, s_in)
-    w1_of, w2_of = (w1t, w1s), (w2t, w2s)
     left, right = pl.ds(0, width // 2), pl.ds(width // 2, width // 2)
     lo, hi = pl.ds(0, half), pl.ds(half, half)
     sib = dp + 1 - 2 * c
 
+    ny2 = ny // 2
+
+    def w1_slot(s):
+        return w1g.at[:, pl.ds(pl.multiple_of(s * hb, hb), hb)]
+
+    def w2_slot(s):
+        return w2g.at[pl.ds(pl.multiple_of(s * hb, hb), hb)]
+
     loads = [
         pltpu.make_async_copy(src, dst, lsem.at[n])
         for n, (src, dst) in enumerate(
-            [(t_in, tok.at[0, rows(me)]), (s_in, tok.at[1, rows(me)]), (w1t_in, w1t), (w2t_in, w2t),
-             (protos_in, protos), (w1s_in, w1s), (w2s_in, w2s)]
+            [(t_in, tok.at[0, rows(c * nx + x)]), (s_in, tok.at[1, rows(me)]), (w1t_in, w1_slot(lax.rem(y, ny2))),
+             (w2t_in, w2_slot(lax.rem(y, ny2))), (protos_in, protos), (w1s_in, w1s), (w2s_in, w2s)]
         )
     ]
-    for load in loads:
-        load.start()
+    for n, load in enumerate(loads):
+        if n not in (2, 3):
+            load.start()
+
+    @pl.when(y // ny2 == c)
+    def _():
+        loads[2].start()
+        loads[3].start()
 
     barrier = pltpu.get_barrier_semaphore()
 
@@ -122,74 +134,143 @@
     loads[1].wait()
     pl.semaphore_wait(barrier, npr - 1 + ndp - 1)
 
-    def tokens_start(v):
-        mine = tok.at[v, rows(me)]
+    def front_start():
+        mine = tok.at[0, rows(c * nx + x)]
         for k in range(1, nx):
-            started(mine, mine, f"tx{v}", dp, proto_of(x + k, y), k)
-        for k in range(1, ny):
-            started(mine, mine, f"ty{v}", dp, proto_of(x, y + k), k)
-
-    def tokens_forward(v):
-        for k in range(1, max(nx, ny)):
-            if k < nx:
-                block = rows(proto_of(x - k, y))
-                arrived(tok.at[v, block], f"tx{v}", k)
-                ref = tok.at[v, block, left]
-                for m in range(1, ny):
-                    started(ref, ref, f"fa{v}", dp, proto_of(x, y + m))
-            if k < ny:
-                block = rows(proto_of(x, y - k))
-                arrived(tok.at[v, block], f"ty{v}", k)
-                ref = tok.at[v, block, right]
-                for m in range(1, nx):
-                    started(ref, ref, f"fb{v}", dp, proto_of(x + m, y))
-
-    diagonal = pl.ds(0, (nx - 1) * (ny - 1) * rb)
-
-    def tokens_wait(v):
-        arrived(tok.at[v, diagonal, left], f"fa{v}")
-        arrived(tok.at[v, diagonal, right], f"fb{v}")
-
-    def tokens_drain(v):
-        gone(tok.at[v, pl.ds(0, (nx - 1) * rb)], f"tx{v}")
-        gone(tok.at[v, pl.ds(0, (ny - 1) * rb)], f"ty{v}")
-        gone(tok.at[v, diagonal, left], f"fa{v}")
-        gone(tok.at[v, diagonal, right], f"fb{v}")
-
-    def head(v):
-        step = min(group, 256)
-
-        def chunk(i):
-            r = pl.ds(pl.multiple_of(i * step, step), step)
-            pre = jnp.dot(tok[v, r, :], w1_of[v][...], preferred_element_type=F32)
-            hidden = gelu(pre).astype(BF16)
-            if v == 1:
-                pre_s[r, :] = pre
-                hid_s[r, :] = hidden
-            rawp[v, r, :] = jnp.dot(hidden, w2_of[v][...], preferred_element_type=F32)
-
-        loop(0, group // step, chunk, unroll=group // step)
-
-    def raw_send(v):
-        def send(k):
-            to = ring(me + k, npr)
-            started(rawp.at[v, rows(to)], rawr.at[v, k], f"rr{v}", dp, to)
-
-        loop(1, npr, send)
-
-    others = pl.ds(1, npr - 1)
-
-    def raw_finish(v):
-        arrived(rawr.at[v, others], f"rr{v}")
-        raw = rawp[v, rows(me), :]
-        for k in range(1, npr):
-            raw = raw + rawr[v, k]
+            started(mine, mine, "tx0", dp, proto_of(x + k, y), k)
+        started(mine, mine, "ts0", sib, me)
+
+        @pl.when(y // ny2 == c)
+        def _():
+            s = lax.rem(y, ny2)
+            loads[2].wait()
+            for k in range(1, ny):
+                started(w1_slot(s), w1_slot(s), "v1", dp, proto_of(x, y + k), s, f"v1s{k}")
+            loads[3].wait()
+            for k in range(1, ny):
+                started(w2_slot(s), w2_slot(s), "v2", dp, proto_of(x, y + k), s, f"v2s{k}")
+
+    def front_forward():
+        for k in range(1, nx):
+            block = tok.at[0, rows(c * nx + lax.rem(x - k + nx, nx))]
+            arrived(block, "tx0", k)
+            started(block, block, "ts0", sib, me)
+
+    def front_wait():
+        arrived(tok.at[0, pl.ds(pl.multiple_of((1 - c) * (nx * rb), nx * rb), nx * rb)], "ts0")
+        for s in range(ny2):
+
+            @pl.when(c * ny2 + s != y)
+            def _(s=s):
+                arrived(w1_slot(s), "v1", s)
+                arrived(w2_slot(s), "v2", s)
+
+    def front_drain():
+        gone(tok.at[0, pl.ds(0, (nx - 1) * rb)], "tx0")
+        gone(tok.at[0, pl.ds(0, nx * rb)], "ts0")
+
+        @pl.when(y // ny2 == c)
+        def _():
+            for k in range(1, ny):
+                gone(w1_slot(0), f"v1s{k}")
+                gone(w2_slot(0), f"v2s{k}")
+
+    def front_head():
+        r = pl.ds(0, 2 * nx * rb)
+        pre = jnp.dot(tok[0, r, :], w1g[...], preferred_element_type=F32)
+        rawp[0, r, :] = jnp.dot(gelu(pre).astype(BF16), w2g[...], preferred_element_type=F32)
+
+    def front_raw_send():
+        for kc in range(2):
+            for kx in range(nx):
+                if kc or kx:
+                    cc, xx = c + kc - 2 * c * kc, lax.rem(x + kx, nx)
+                    started(rawp.at[0, rows(cc * nx + xx)], rawr.at[0, kc * nx + kx], "rr0", 2 * z + cc, proto_of(xx, y))
+
+    def front_raw_finish():
+        arrived(rawr.at[0, pl.ds(1, 2 * nx - 1)], "rr0")
+        raw = rawp[0, rows(c * nx + x), :]
+        for k in range(1, 2 * nx):
+            raw = raw + rawr[0, k]
+        put_unit(0, raw)
+
+    def front_raw_drain():
+        gone(rawr.at[0, pl.ds(1, 2 * nx - 1)], "rr0")
+
+    def put_unit(v, raw):
         scale = unit_scale(raw)
         unit_float = raw * scale
         if v == 1:
             own_float[...] = unit_float
             own_scale[...] = scale
         units[v, z, c, :, hrows(me), :] = unit_float.astype(BF16).reshape(2, hr, cols)
+
+    def tokens_start_x(v):
+        mine = tok.at[v, rows(me)]
+        for k in range(1, nx):
+            started(mine, mine, f"tx{v}", dp, proto_of(x + k, y), k)
+
+    def tokens_start_y(v):
+        mine = tok.at[v, rows(me)]
+        for k in range(1, ny):
+            started(mine, mine, f"ty{v}", dp, proto_of(x, y + k), k)
+
+    def tokens_forward_y(v):
+        for k in range(1, nx):
+            block = rows(proto_of(x - k, y))
+            arrived(tok.at[v, block], f"tx{v}", k)
+            ref = tok.at[v, block, left]
+            for m in range(1, ny):
+                started(ref, ref, f"fa{v}", dp, proto_of(x, y + m))
+
+    def tokens_forward_x(v):
+        for k in range(1, ny):
+            block = rows(proto_of(x, y - k))
+            arrived(tok.at[v, block], f"ty{v}", k)
+            ref = tok.at[v, block, right]
+            for m in range(1, nx):
+                started(ref, ref, f"fb{v}", dp, proto_of(x + m, y))
+
+    diagonal = pl.ds(0, (nx - 1) * (ny - 1) * rb)
+
+    def tokens_wait(v):
+        arrived(tok.at[v, diagonal, left], f"fa{v}")
+        arrived(tok.at[v, diagonal, right], f"fb{v}")
+
+    def tokens_drain(v):
+        gone(tok.at[v, pl.ds(0, (nx - 1) * rb)], f"tx{v}")
+        gone(tok.at[v, pl.ds(0, (ny - 1) * rb)], f"ty{v}")
+        gone(tok.at[v, diagonal, left], f"fa{v}")
+        gone(tok.at[v, diagonal, right], f"fb{v}")
+
+    def head(v):
+        step = min(group, 256)
+
+        def chunk(i):
+            r = pl.ds(pl.multiple_of(i * step, step), step)
+            pre = jnp.dot(tok[v, r, :], w1s[...], preferred_element_type=F32)
+            hidden = gelu(pre).astype(BF16)
+            pre_s[r, :] = pre
+            hid_s[r, :] = hidden
+            rawp[v, r, :] = jnp.dot(hidden, w2s[...], preferred_element_type=F32)
+
+        loop(0, group // step, chunk, unroll=group // step)
+
+    def raw_send(v):
+        def send(k):
+            to = ring(me + k, npr)
+            started(rawp.at[v, rows(to)], rawr.at[v, k], f"rr{v}", dp, to)
+
+        loop(1, npr, send)
+
+    others = pl.ds(1, npr - 1)
+
+    def raw_finish(v):
+        arrived(rawr.at[v, others], f"rr{v}")
+        raw = rawp[v, rows(me), :]
+        for k in range(1, npr):
+            raw = raw + rawr[v, k]
+        put_unit(v, raw)
 
     def raw_drain(v):
         gone(rawr.at[v, others], f"rr{v}")
@@ -257,6 +338,52 @@
         gone(units.at[v, pl.ds(0, nz - 1), c, 1, :, lo], f"a2{v}")
         gone(units.at[v, :, c, 1, :, lo], f"sa{v}")
         gone(units.at[v, :, c, 1, :, hi], f"sb{v}")
+
+    def slow_first(v):
+        mine = units.at[v, z, c, :, hrows(me)]
+        for k in range(1, nz):
+            started(mine.at[:, :, hi], mine.at[:, :, hi], f"b1{v}", ring(z + k, nz) * 2 + c, me)
+        loop(1, npr, lambda k: started(mine.at[:, :, lo], mine.at[:, :, lo], f"a1{v}", dp, ring(me + k, npr)))
+
+    def slow_second_z(v):
+        arrived(units.at[v, z, c, :, pl.ds(0, (npr - 1) * hr), lo], f"a1{v}")
+        plane = units.at[v, z, c, :, :, lo]
+        for k in range(1, nz):
+            started(plane, plane, f"a2{v}", ring(z + k, nz) * 2 + c, me, k)
+        started(plane, plane, f"sa{v}", sib, me)
+
+    def slow_second_proto(v):
+        arrived(units.at[v, pl.ds(0, nz - 1), c, :, hrows(me), hi], f"b1{v}")
+        col = units.at[v, :, c, :, hrows(me), hi]
+        for kx in range(nx):
+            for ky in range(ny):
+                if kx or ky:
+                    started(col, col, f"b2{v}", dp, proto_of(x + kx, y + ky), kx)
+
+    def slow_third(v):
+        for k in range(1, nz):
+            plane = units.at[v, ring(z - k, nz), c, :, :, lo]
+            arrived(plane, f"a2{v}", k)
+            started(plane, plane, f"sa{v}", sib, me)
+        for k in range(nx):
+            piece = units.at[v, :, c, :, band(x - k), hi]
+            if k:
+                arrived(piece, f"b2{v}", k)
+            else:
+                arrived(units.at[v, :, c, :, pl.ds(0, (ny - 1) * hr), hi], f"b2{v}", k)
+            started(piece, piece, f"sb{v}", sib, me)
+
+    def slow_wait(v):
+        arrived(units.at[v, :, 1 - c, :, :, lo], f"sa{v}")
+        arrived(units.at[v, :, 1 - c, :, :, hi], f"sb{v}")
+
+    def slow_drain(v):
+        gone(units.at[v, z, c, :, pl.ds(0, (npr - 1) * hr), lo], f"a1{v}")
+        gone(units.at[v, pl.ds(0, nz - 1), c, :, hrows(me), hi], f"b1{v}")
+        gone(units.at[v, :, c, :, pl.ds(0, (npr - 1) * hr), hi], f"b2{v}")
+        gone(units.at[v, pl.ds(0, nz - 1), c, :, :, lo], f"a2{v}")
+        gone(units.at[v, :, c, :, :, lo], f"sa{v}")
+        gone(units.at[v, :, c, :, :, hi], f"sb{v}")
 
     pb = min(kp, 256)
     nb = kp // pb
@@ -366,46 +493,49 @@
     def next_weight(v):
         return 1.0 / (crops * v)
 
-    tokens_start(0)
+    front_start()
+    tokens_start_x(1)
+    tokens_start_y(1)
     ps1[...] = jnp.zeros_like(ps1)
     colb[...] = jnp.zeros_like(colb)
-    for load in loads[2:]:
+    for load in loads[4:]:
         load.wait()
-    tokens_forward(0)
+    front_forward()
     ptr[...] = protos[...].astype(F32).T.astype(BF16)
-    tokens_wait(0)
-    head(0)
-    raw_send(0)
-    raw_finish(0)
+    front_wait()
+    front_head()
+    front_raw_send()
+    tokens_forward_y(1)
+    tokens_forward_x(1)
+    front_raw_finish()
     ag_first(0)
-    tokens_start(1)
     ag_second(0)
-    tokens_forward(1)
+    tokens_wait(1)
+    head(1)
     ag_third(0)
+    raw_send(1)
     teacher_scores(c)
     ag_wait(0)
     teacher_scores(1 - c)
-    tokens_wait(1)
-    head(1)
-    raw_send(1)
     first_scales()
     row_pass(False)
     put_rows(0, 0)
     sum_send(0)
+    raw_finish(1)
+    slow_first(1)
     sum_middle(0)
-    raw_finish(1)
-    ag_first(1)
+    slow_second_z(1)
     sum_finish(0)
     spread(0, 0, next_weight, 0)
+    slow_second_proto(1)
     row_pass(True)
     put_rows(1, 0)
     sum_send(1)
-    ag_second(1)
     sum_middle(1)
-    ag_third(1)
+    slow_third(1)
     rows8[...] = jnp.zeros_like(rows8)
     student_scores(c)
-    ag_wait(1)
+    slow_wait(1)
     student_scores(1 - c)
     put_rows(2, 1)
     sum_finish(1)
@@ -541,9 +671,9 @@
             gw[sl, :] = tn_dot(tok[1, :, sl], pre_grad)
             done = (i + 1) * wchunk
         else:
-            w2g = tn_dot(hid_s[...], raw_grad)
-            gw[pl.ds(width, hb), :] = w2g[:, :hb]
-            gw[pl.ds(width + hb, hb), :] = w2g[:, hb:]
+            grad2 = tn_dot(hid_s[...], raw_grad)
+            gw[pl.ds(width, hb), :] = grad2[:, :hb]
+            gw[pl.ds(width + hb, hb), :] = grad2[:, hb:]
             done = whole
         while sent < parts and done >= 2 * (sent + 1) * share_rows:
             started(gw.at[half_of(sent, 1 - c)], gwr.at[sent], "w0", sib, me, sent)
@@ -574,10 +704,12 @@
         loss = loss + lossdr[k]
     loss_out[...] = jnp.sum(jnp.sum(loss, axis=0, keepdims=True), axis=1, keepdims=True)
 
-    for v in (0, 1):
-        tokens_drain(v)
-        raw_drain(v)
-        ag_drain(v)
+    front_drain()
+    front_raw_drain()
+    tokens_drain(1)
+    raw_drain(1)
+    ag_drain(0)
+    slow_drain(1)
     for t in range(3):
         sum_drain(t)
     gone(sibs, "g0")
@@ -613,7 +745,9 @@
 
     plan, n_send, n_recv = {}, 0, 0
     phases = [(f"{name}{v}", n) for v in (0, 1) for name, n in dict(
-        tx=nx, ty=ny, fa=1, fb=1, rr=1, a1=1, b1=1, b2=nx, a2=nz, d1=nz, sa=1, sb=1, sd=1).items()]
+        rr=1, a1=1, b1=1, b2=nx, a2=nz, d1=nz, sa=1, sb=1, sd=1).items()]
+    phases += [("tx0", nx), ("ts0", 1), ("v1", ny // 2), ("v2", ny // 2), ("tx1", nx), ("ty1", ny), ("fa1", 1), ("fb1", 1)]
+    phases += [(f"{name}s{k}", 0) for name in ("v1", "v2") for k in range(1, ny)]
     phases += [(f"{name}{t}", 1) for t in range(3) for name in ("s1", "s2")]
     phases += [("g0", nz), ("gz", 2), ("w0", 2), ("w1", 2), ("w2", 2)]
     phases += [(n, 1) for n in ("gp", "go", "ga", "gb", "l1", "l2", "r1", "w3")]
@@ -627,8 +761,8 @@
     scratch = [
         V((width, hb), BF16),
         V((hb, cols), BF16),
-        V((width, hb), BF16),
-        V((hb, cols), BF16),
+        V((width, ny // 2 * hb), BF16),
+        V((ny // 2 * hb, cols), BF16),
         V((kp, cols), BF16),
         V((2, group, width), BF16),
         V((group, hb), F32),

time: 149 us -> 142 us (0.953)
  Pallas kernels: 144 us -> 137 us
    pallas_call x1, Pallas kernels: 144 us -> 137 us  [step(): pl.pallas_call(functools.partial(kernel, dims, plan), out_shape=(pltpu.VM...]
where the time goes in v4:
time: 142 us
  Pallas kernels  137 us (96%)
  local copies, waits for them, and re-layouts  2.51 us (2%)
  between operations  2.33 us (2%)
    pallas_call x1, Pallas kernels, step(): pl.pallas_call(functools.partial(kernel, dims, plan), out_shape=(pltpu.VM...  137 us

profile of v4, /device:TPU:1, one launch (start us, length us, event | category | flops | bytes accessed | tf_op | source)
XLA Modules:
  0.0 142.3 jit_solution(12601077099691393052)
XLA Ops:
  0.6 137.5 %shard_map.102 = (f32[1024,256]{1,0:T(8,128)S(1)}, f32[1536,128]{1,0:T(8,128)S(1)}, f32[128,256]{1,0:T(8,128)S(1)}, f32[1,1]{1,0:T(1,128)}) custom-call(bf16[32,1536]{1,0:T(8,128)(2,1)} %s_in.1, bf16[32,1536]{1,0:T(8,128)(2,1)} %t_in.1, bf16[1536,128]{1,0:T(8,128)(2,1)} %w1s_in.1, bf16[128,256]{1,0:T(8,128)(2,1)} %w2s_in.1, bf16[1536,128]{1,0:T(8,128)(2,1)} %w1t_in.1, ...), custom_call_target="tpu_custom_call" | custom-call | flops 8589934592 | bytes 4194304 | tf_op jit(solution)/shard_map/pallas_call | solution.py:812
  138.1 1.0 copy.15
  139.1 0.7 copy.17
  139.8 0.9 copy.16

commit v5 on v4

--- a/solution.py
+++ b/solution.py
@@ -73,7 +73,12 @@
     def gone(src, name):
         pltpu.make_async_copy(src, src, ssem.at[plan[name][0]]).wait()
 
-    def loop(lo, hi, fn, unroll=1):
+    def loop(lo, hi, fn, unroll=None):
+        if unroll is None:
+            for k in range(lo, hi):
+                fn(k)
+            return
+
         def step(k, carry):
             fn(k)
             return carry
@@ -312,6 +317,8 @@
             else:
                 arrived(units.at[v, z, c, 0, pl.ds(0, (npr - 1) * hr)], f"d1{v}", k)
             started(plane, plane, f"sd{v}", sib, me)
+
+    def ag_fourth(v):
         for k in range(1, nz):
             plane = units.at[v, ring(z - k, nz), c, 1, :, lo]
             arrived(plane, f"a2{v}", k)
@@ -324,8 +331,10 @@
                 arrived(units.at[v, :, c, 1, pl.ds(0, (ny - 1) * hr), hi], f"b2{v}", k)
             started(piece, piece, f"sb{v}", sib, me)
 
+    def ag_wait_straight(v):
+        arrived(units.at[v, :, 1 - c, 0], f"sd{v}")
+
     def ag_wait(v):
-        arrived(units.at[v, :, 1 - c, 0], f"sd{v}")
         arrived(units.at[v, :, 1 - c, 1, :, lo], f"sa{v}")
         arrived(units.at[v, :, 1 - c, 1, :, hi], f"sb{v}")
 
@@ -389,19 +398,21 @@
     nb = kp // pb
     gtiles = group // 128
 
-    def teacher_scores(cc):
+    def teacher_scores(cc, h):
+        wide = group // 2
+
         def step(i):
             zz, b = i // nb, i % nb
             r = pl.ds(pl.multiple_of(b * pb, pb), pb)
-            s = nt_dot(protos[r, :], units[0, zz, cc].reshape(group, cols))
+            s = nt_dot(protos[r, :], units[0, zz, cc, h])
             e = jnp.exp2(s * (LOG2E / TEACHER_TEMP))
-            ex[r, pl.ds(pl.multiple_of((2 * zz + cc) * group, group), group)] = e
+            ex[r, pl.ds(pl.multiple_of((2 * zz + cc) * group + h * wide, wide), wide)] = e
             acc = e[:, :128]
-            for j in range(1, gtiles):
+            for j in range(1, wide // 128):
                 acc = acc + e[:, j * 128 : (j + 1) * 128]
             colb[r, :] += acc
 
-        loop(0, nz * nb, step, unroll=2 * nb)
+        loop(0, nz * nb, step, unroll=4 * nb)
 
     def first_scales():
         def scale(i):
@@ -513,10 +524,14 @@
     tokens_wait(1)
     head(1)
     ag_third(0)
+    teacher_scores(c, 0)
+    ag_fourth(0)
     raw_send(1)
-    teacher_scores(c)
+    ag_wait_straight(0)
+    teacher_scores(1 - c, 0)
+    teacher_scores(c, 1)
     ag_wait(0)
-    teacher_scores(1 - c)
+    teacher_scores(1 - c, 1)
     first_scales()
     row_pass(False)
     put_rows(0, 0)
@@ -559,20 +574,25 @@
         def step(b):
             base = pl.multiple_of(b * pb, pb)
             r = pl.ds(base, pb)
-            lossa = jnp.zeros((8, 128), F32)
-            for j in range(gtiles):
-                lanes = pl.ds(pl.multiple_of(lane0 + j * 128, 128), 128)
-                inv, norm = wb[0:8, lanes], wb[8:16, lanes]
-                for a in range(0, pb, 16):
+            lanes = [pl.ds(pl.multiple_of(lane0 + j * 128, 128), 128) for j in range(gtiles)]
+            inv = [wb[0:8, l] for l in lanes]
+            norm = [wb[8:16, l] for l in lanes]
+            lossa = [jnp.zeros((8, 128), F32) for _ in range(2 * gtiles)]
+            for a in range(0, pb, 16):
+                scale = [colb[pl.ds(base + a + h, 8), :] for h in (0, 8)]
+                for j in range(gtiles):
                     outs = []
-                    for h in (0, 8):
-                        rr = pl.ds(base + a + h, 8)
-                        tgt = ex[rr, lanes] * colb[rr, :] * inv
-                        rel = lg2[rr, lanes] - norm
-                        lossa = lossa - tgt * rel
+                    for h in range(2):
+                        rr = pl.ds(base + a + 8 * h, 8)
+                        tgt = ex[rr, lanes[j]] * scale[h] * inv[j]
+                        rel = lg2[rr, lanes[j]] - norm[j]
+                        lossa[2 * j + h] = lossa[2 * j + h] - tgt * rel
                         outs.append((jnp.exp2(rel) - tgt) * share)
                     gt[pl.ds(base + a, 16), j * 128 : (j + 1) * 128] = jnp.concatenate(outs, axis=0).astype(BF16)
-            losst[...] += lossa
+            total = lossa[0]
+            for term in lossa[1:]:
+                total = total + term
+            losst[...] += total
             gp_out[r, :] += jnp.dot(gt[r, :], u, preferred_element_type=F32)
 
         loop(0, nb, step, unroll=nb)
@@ -730,6 +750,27 @@
     gw2_out[:, :hb] = fw[width : width + hb, :]
     gw2_out[:, hb:] = fw[width + hb :, :]
     gone(gwr, "w3")
+
+
+def copy_kernel(*refs):
+    n = len(refs) // 2
+    copies = [pltpu.make_async_copy(refs[i], refs[n + i], refs[-1].at[i]) for i in range(n)]
+    for copy in copies:
+        copy.start()
+    for copy in copies:
+        copy.wait()
+
+
+def write_out(*arrays):
+    anywhere = pl.BlockSpec(memory_space=pl.ANY)
+    return pl.pallas_call(
+        copy_kernel,
+        out_shape=tuple(jax.ShapeDtypeStruct(a.shape, a.dtype) for a in arrays),
+        in_specs=[anywhere] * len(arrays),
+        out_specs=(anywhere,) * len(arrays),
+        scratch_shapes=[pltpu.SemaphoreType.DMA((len(arrays),))],
+        cost_estimate=pl.CostEstimate(flops=0, bytes_accessed=8 * sum(a.size for a in arrays), transcendentals=0),
+    )(*arrays)
 
 
 def step(dims, s_in, t_in, w1s, w2s, w1t, w2t, protos):
@@ -827,6 +868,7 @@
             flops=8 * kp * crops * cols, bytes_accessed=4 * kp * cols * 4, transcendentals=2 * kp * crops
         ),
     )(s_in, t_in, w1s, w2s, w1t, w2t, protos)
+    gp, gw1, gw2 = write_out(gp, gw1, gw2)
     return gp, gw1, gw2, loss[0, 0]
 
 

time: 142 us -> 203 us (1.43)
  Pallas kernels: 137 us -> 198 us
    pallas_call x0 -> x1, Pallas kernels: none -> 60.7 us  [write_out(): pl.pallas_call(copy_kernel, out_shape=tuple((jax.ShapeDtypeStruct(a.shape...]
where the time goes in v5:
time: 203 us
  Pallas kernels  198 us (98%)
  local copies, waits for them, and re-layouts  2.54 us (1%)
  between operations  2.33 us (1%)
    pallas_call x1, Pallas kernels, step(): pl.pallas_call(functools.partial(kernel, dims, plan), out_shape=(pltpu.VM...  137 us
    pallas_call x1, Pallas kernels, write_out(): pl.pallas_call(copy_kernel, out_shape=tuple((jax.ShapeDtypeStruct(a.shape...  60.7 us

profile of v5, /device:TPU:1, one launch (start us, length us, event | category | flops | bytes accessed | tf_op | source)
XLA Modules:
  0.0 202.7 jit_solution(1665067038603334089)
XLA Ops:
  0.6 137.1 %shard_map.102 = (f32[1024,256]{1,0:T(8,128)S(1)}, f32[1536,128]{1,0:T(8,128)S(1)}, f32[128,256]{1,0:T(8,128)S(1)}, f32[1,1]{1,0:T(1,128)}) custom-call(bf16[32,1536]{1,0:T(8,128)(2,1)} %s_in.1, bf16[32,1536]{1,0:T(8,128)(2,1)} %t_in.1, bf16[1536,128]{1,0:T(8,128)(2,1)} %w1s_in.1, bf16[128,256]{1,0:T(8,128)(2,1)} %w2s_in.1, bf16[1536,128]{1,0:T(8,128)(2,1)} %w1t_in.1, ...), custom_call_target="tpu_custom_call" | custom-call | flops 8589934592 | bytes 4194304 | tf_op jit(solution)/shard_map/pallas_call | solution.py:853
  137.7 0.0 copy-start
  137.7 1.0 copy-done
  138.7 0.0 copy-start.1
  138.7 0.9 copy-done.1
  139.6 0.0 copy-start.2
  139.6 0.7 copy-done.2
  140.3 60.7 %shard_map.103 = (f32[1024,256]{1,0:T(8,128)}, f32[1536,128]{1,0:T(8,128)}, f32[128,256]{1,0:T(8,128)}) custom-call(f32[1024,256]{1,0:T(8,128)} %copy-done, f32[1536,128]{1,0:T(8,128)} %copy-done.1, f32[128,256]{1,0:T(8,128)} %copy-done.2), custom_call_target="tpu_custom_call" | custom-call | bytes 3932160 | tf_op jit(solution)/shard_map/pallas_call | solution.py:766
Async XLA Ops:
  137.7 1.0 copy-start
  138.7 0.9 copy-start.1
  139.6 0.7 copy-start.2
